TPU v7x, 128 devices: a whole 4x4x4 slice. The times are simulated.
128 devices in a mesh: dp: 16 (over x, z), tensor: 8 (over y, core).
Axes of the slice: x: 4, y: 4, z: 4, core: 2. Of those that a mesh axis runs over, the one named last changes fastest.
Arguments:
- conv_input: bfloat16 [96, 96, 16384], P('dp', None, 'tensor'), may hold values from -6 to 6
- gate_input: bfloat16 [96, 96, 16384], P('dp', None, 'tensor'), may hold values from -6 to 6
- conv_weight: float32 [4, 16384], P(None, 'tensor'), may hold values from -3 to 3
- conv_bias: float32 [16384], P('tensor'), may hold values from -3 to 3
- state_pool: float32 [2048, 19456], P('dp', 'tensor'), may hold values from -6 to 6
- page_owner: int32 [96, 16, 1], P('dp'), may hold values from 0 to 15; in each aligned block of 96 rows (0 to 95, 96 to 191, ..., all dimensions but the last counted through in order) at most 9 rows name the same one
- page_slot: int32 [96, 16], P('dp'), may hold values from 0 to 127
- page_count: int32 [96], P('dp'), may hold values from 1 to 16
- step_in_weight: bfloat16 [16384, 512], P('tensor'), may hold values from -0.046875 to 0.046875
- coupling_weight: bfloat16 [32, 16384], P(None, 'tensor'), may hold values from -0.046875 to 0.046875
- step_gain: float32 [512], replicated, may hold values from 0.1 to 1.9
- step_weight: bfloat16 [512, 16384], P(None, 'tensor'), may hold values from -0.25 to 0.25
- step_bias: float32 [16384], P('tensor'), may hold values from -5 to -1
- decay_log: float32 [16, 16384], P(None, 'tensor'), may hold values from 0 to 2.8
- skip_gain: float32 [16384], P('tensor'), may hold values from 0.5 to 1.5
- out_weight: bfloat16 [16384, 4096], P('tensor', 'dp'), may hold values from -0.046875 to 0.046875
Outputs:
- mixer_out: bfloat16 [96, 96, 4096], P('dp', None, 'tensor')
- final_state: float32 [96, 16, 16384], P('dp', None, 'tensor')
Inputs may be any that keep to these rules, and one draw needn't show every extreme that they name: `page_owner`: among the pages listed for the 6 sessions of one dp index, at most 9 name the same owner. `page_slot`: several pages may name the same row. `page_count`: pages at list positions from the count on were never stored and hold zero state, whatever the lists name there.
All inputs are finite; a program needn't handle non-finite values.
Results may differ from a plain program's by a relative error of at most 0.018.
Values may be sent and summed in bfloat16 or wider, within the bound.
A program may use at most 128 MiB of HBM per device.

v0:
```python
import jax
import jax.numpy as jnp
from jax import lax
from jax.sharding import PartitionSpec as P

EPSILON = 1e-06


def body(
    conv_input,
    gate_input,
    conv_weight,
    conv_bias,
    state_pool,
    page_owner,
    page_slot,
    page_count,
    step_in_weight,
    coupling_weight,
    step_gain,
    step_weight,
    step_bias,
    decay_log,
    skip_gain,
    out_weight,
):
    sess_here, new_len, chan_here = conv_input.shape
    page_total = page_slot.shape[1]
    pool_depth = state_pool.shape[0]
    state_width = decay_log.shape[0]
    tap_count = conv_weight.shape[0]
    page_chan = chan_here // page_total
    entry_width = state_pool.shape[1] // page_chan
    owners = page_owner[:, :, 0].reshape(-1)
    slot_ids = page_slot.reshape(-1)
    wanted = owners * pool_depth + slot_ids
    row_block = lax.all_gather(state_pool, "dp", axis=0, tiled=True)
    inside = (wanted >= 0) & (wanted < row_block.shape[0])
    chosen = jnp.take(row_block, jnp.clip(wanted, 0, row_block.shape[0] - 1), axis=0)
    fetched = jnp.where(inside[:, None], chosen, 0.0)
    stored = (jnp.arange(page_total, dtype=jnp.int32)[None, :] < page_count[:, None]).astype(
        jnp.float32
    )
    fetched = (
        fetched.reshape(sess_here, page_total, page_chan, entry_width) * stored[:, :, None, None]
    )
    unpacked = jnp.transpose(fetched, (0, 3, 1, 2)).reshape(sess_here, entry_width, chan_here)
    start_state = unpacked[:, :state_width]
    conv_history = unpacked[:, state_width:]
    history = jnp.concatenate([conv_history, conv_input.astype(jnp.float32)], axis=1)
    pre_act = conv_bias
    for tap_index in range(tap_count):
        pre_act = pre_act + conv_weight[tap_index] * history[:, tap_index : tap_index + new_len]
    signal = jax.nn.silu(pre_act)
    signal_low = signal.astype(jnp.bfloat16).reshape(sess_here * new_len, chan_here)
    step_part = jnp.dot(signal_low, step_in_weight, preferred_element_type=jnp.float32)
    coupling_part = lax.dot_general(
        signal_low, coupling_weight, (((1,), (1,)), ((), ())), preferred_element_type=jnp.float32
    )
    step_low, coupling = lax.psum((step_part, coupling_part), "tensor")
    inv_rms = lax.rsqrt(jnp.mean(step_low * step_low, axis=-1, keepdims=True) + EPSILON)
    step_normed = (step_low * inv_rms * step_gain).astype(jnp.bfloat16)
    step_size = jax.nn.softplus(
        jnp.dot(step_normed, step_weight, preferred_element_type=jnp.float32) + step_bias
    )
    decay_rate = -jnp.exp(decay_log)

    def by_time(values):
        return jnp.swapaxes(values.reshape(sess_here, new_len, -1), 0, 1)

    def advance(carried, inputs_now):
        step_now, signal_now, b_now, c_now = inputs_now
        carried = (
            jnp.exp(step_now[:, None, :] * decay_rate[None]) * carried
            + (step_now * signal_now)[:, None, :] * b_now[:, :, None]
        )
        result = jnp.sum(c_now[:, :, None] * carried, axis=1) + skip_gain * signal_now
        return (carried, result)

    scan_inputs = (
        by_time(step_size),
        jnp.swapaxes(signal, 0, 1),
        by_time(coupling[:, :state_width]),
        by_time(coupling[:, state_width:]),
    )
    final_state, outputs = lax.scan(advance, start_state, scan_inputs, unroll=8)
    gated_out = (jnp.swapaxes(outputs, 0, 1) * jax.nn.silu(gate_input.astype(jnp.float32))).astype(
        jnp.bfloat16
    )
    gated_out = gated_out.reshape(sess_here * new_len, chan_here)
    partials = jnp.dot(
        gated_out,
        lax.all_gather(out_weight, "dp", axis=1, tiled=True),
        preferred_element_type=jnp.float32,
    )
    summed = lax.psum_scatter(
        partials.astype(jnp.bfloat16), "tensor", scatter_dimension=1, tiled=True
    )
    mixer_out = summed.reshape(sess_here, new_len, -1)
    return (mixer_out, final_state)


def solution(mesh):
    return jax.shard_map(
        body,
        mesh=mesh,
        in_specs=(
            P("dp", None, "tensor"),
            P("dp", None, "tensor"),
            P(None, "tensor"),
            P("tensor"),
            P("dp", "tensor"),
            P("dp", None, None),
            P("dp", None),
            P("dp"),
            P("tensor", None),
            P(None, "tensor"),
            P(),
            P(None, "tensor"),
            P("tensor"),
            P(None, "tensor"),
            P("tensor"),
            P("tensor", "dp"),
        ),
        out_specs=(P("dp", None, "tensor"), P("dp", None, "tensor")),
        check_vma=False,
    )
```

profile of v0, /device:TPU:5, one launch (start us, length us, event | category | flops | bytes accessed | tf_op | source)
XLA Modules:
  0.0 513.2 jit_solution(2256649054319431407)
XLA Ops:
  9.5 4.4 convert_element_type.26
  14.1 126.0 %all-gather.3.cloned.1.call-done = f32[2048,2432]{1,0:T(8,128)} async-done(((f32[128,2432]{1,0:T(8,128)}), f32[2048,2432]{1,0:T(8,128)}) %all-gather.3.cloned.1.call-update) | async-done | bytes 19922960 | tf_op jit(solution)/shard_map/all_gather | solution.py:37
  140.1 8.0 %gather_fusion = f32[96,2432]{1,0:T(8,128)S(1)} fusion(f32[2048,2432]{1,0:T(8,128)} %all-gather.3.cloned.1.call-done, s32[1024]{0:T(1024)S(1)} %pad_clamp_fusion), kind=kCustom, calls=%fused_computation | custom fusion | bytes 1868160 | tf_op jit(solution)/shard_map/jit(_take)/gather | solution.py:39
  148.1 8.2 %gather.7 = f32[6,16,128,19]{3,2,1,0:T(8,128)} reshape(f32[96,2432]{1,0:T(8,128)S(1)} %gather_fusion) | data formatting | bytes 1867776 | tf_op jit(solution)/shard_map/jit(_take)/gather | solution.py:39
  156.3 3.3 select_multiply_fusion
  159.6 2.6 copy-done.3
  162.3 4.4 slice.175
  166.6 4.4 copy.46
  171.1 10.1 %fusion.50 = (bf16[6,96,2048]{2,1,0:T(8,128)(2,1)S(1)}, f32[6,96,2048]{2,1,0:T(8,128)}) fusion(f32[6,96,2048]{2,1,0:T(8,128)} %convert_element_type.26, f32[2048]{0:T(1024)S(1)} %bitcast.252, f32[6,3,2048]{2,1,0:T(4,128)S(1)} %copy.46, f32[2048]{0:T(1024)S(1)} %bitcast.253, f32[2048]{0:T(1024)S(1)} %bitcast.251, f32[2048]{0:T(1024)S(1)} %bitcast.250, ...), kind=kLoop, calls=%fused_computation.131 | loop fusion | flops 18874368 | bytes 11984896 | tf_op jit(solution)/shard_map/convert_element_type | solution.py:55
  181.1 2.4 fusion.53
  183.6 1.4 fusion.54
  185.9 7.8 %copy.37 = f32[96,6,2048]{2,1,0:T(8,128)} copy(f32[96,6,2048]{2,0,1:T(8,128)} %bitcast.241) | data formatting | bytes 9437184 | tf_op jit(solution)/shard_map/transpose | solution.py:82
  193.7 4.4 copy.45
  198.1 47.5 %all-reduce.3.cloned.1.call-done = (f32[576,512]{1,0:T(8,128)}, f32[576,32]{0,1:T(8,128)}) async-done(((f32[576,512]{1,0:T(8,128)}, f32[576,32]{0,1:T(8,128)}), (f32[576,512]{1,0:T(8,128)}, f32[576,32]{0,1:T(8,128)})) %all-reduce.3.cloned.1.call-update) | async-done | bytes 1253392 | tf_op jit(solution)/shard_map/psum | solution.py:60
  245.6 1.4 multiply_reduce_fusion.8
  247.1 4.8 compare_select_fusion
  251.9 5.5 %copy.36 = f32[96,6,2048]{2,1,0:T(8,128)} copy(f32[96,6,2048]{2,0,1:T(8,128)S(1)} %bitcast.245) | data formatting | bytes 9437184 | tf_op jit(solution)/shard_map/transpose | solution.py:69
  258.7 186.1 %while.12 = (s32[]{:T(128)}, f32[6,16,2048]{2,1,0:T(8,128)S(1)}, f32[12,8,6,2048]{3,2,1,0:T(8,128)}, f32[12,8,6,2048]{3,2,1,0:T(8,128)}, f32[16,2048]{1,0:T(8,12...) while((s32[]{:T(128)}, f32[6,16,2048]{2,1,0:T(8,128)S(1)}, ...), condition=%wide.region_12.13_spmd, body=%wide.region_3.12_spmd.sunk | while | flops 14352392 | bytes 10491029 | solution.py:86
  258.7 1.5 bitcast_multiply_fusion.17
  261.0 1.1 dynamic-slice_bitcast_fusion.9
  263.2 1.8 multiply_reduce_fusion.12
  265.1 1.5 multiply_reduce_fusion.14
  274.4 1.3 bitcast_multiply_fusion.17
  276.6 1.1 dynamic-slice_bitcast_fusion.9
  278.8 1.8 multiply_reduce_fusion.12
  280.6 1.5 multiply_reduce_fusion.14
  289.9 1.3 bitcast_multiply_fusion.17
  294.2 1.8 multiply_reduce_fusion.12
  296.1 1.5 multiply_reduce_fusion.14
  305.4 1.3 bitcast_multiply_fusion.17
  307.5 1.1 dynamic-slice_bitcast_fusion.9
  309.7 1.8 multiply_reduce_fusion.12
  311.6 1.5 multiply_reduce_fusion.14
  320.8 1.4 bitcast_multiply_fusion.17
  323.0 1.2 dynamic-slice_bitcast_fusion.9
  325.2 1.8 multiply_reduce_fusion.12
  327.1 1.5 multiply_reduce_fusion.14
  336.4 1.3 bitcast_multiply_fusion.17
  340.7 1.8 multiply_reduce_fusion.12
  342.6 1.5 multiply_reduce_fusion.14
  351.9 1.4 bitcast_multiply_fusion.17
  354.1 1.1 dynamic-slice_bitcast_fusion.9
  356.3 1.8 multiply_reduce_fusion.12
  358.2 1.5 multiply_reduce_fusion.14
  367.4 1.3 bitcast_multiply_fusion.17
  371.8 1.8 multiply_reduce_fusion.12
  373.6 1.5 multiply_reduce_fusion.14
  382.9 1.3 bitcast_multiply_fusion.17
  385.1 1.1 dynamic-slice_bitcast_fusion.9
  387.2 1.8 multiply_reduce_fusion.12
  389.1 1.5 multiply_reduce_fusion.14
  398.4 1.3 bitcast_multiply_fusion.17
  400.5 1.1 dynamic-slice_bitcast_fusion.9
  402.7 1.8 multiply_reduce_fusion.12
  404.6 1.5 multiply_reduce_fusion.14
  413.9 1.3 bitcast_multiply_fusion.17
  418.2 1.8 multiply_reduce_fusion.12
  420.1 1.5 multiply_reduce_fusion.14
  429.3 1.3 bitcast_multiply_fusion.17
  433.7 1.8 multiply_reduce_fusion.12
  435.5 1.5 multiply_reduce_fusion.14
  444.8 8.3 %fusion.45 = bf16[6,96,2048]{2,1,0:T(8,128)(2,1)} fusion(bf16[6,96,2048]{2,1,0:T(8,128)(2,1)} %param.19, f32[96,6,2048]{2,1,0:T(8,128)} %bitcast.244), kind=kLoop, calls=%fused_computation.114 | loop fusion | flops 8257536 | bytes 9437184 | tf_op jit(solution)/shard_map/convert_element_type | solution.py:87
  453.1 15.8 %convolution_convert_fusion = bf16[576,4096]{1,0:T(8,128)(2,1)} fusion(bf16[576,2048]{1,0:T(8,128)(2,1)} %bitcast.246, bf16[2048,4096]{1,0:T(8,128)(2,1)} %all-gather.5.cloned.1.call-done), kind=kOutput, calls=%fused_computation.94 | convolution fusion | flops 9666035712 | bytes 23855104 | tf_op jit(solution)/shard_map/dot_general | solution.py:91
  468.9 37.8 %reduce-scatter.2.cloned.1.call-done = bf16[576,512]{1,0:T(8,128)(2,1)} async-done(((bf16[576,4096]{1,0:T(8,128)(2,1)}), bf16[576,512]{1,0:T(8,128)(2,1)}) %reduce-scatter.2.cloned.1.call-update) | async-done | bytes 589840 | tf_op jit(solution)/shard_map/reduce_scatter | solution.py:96
  (192 shorter events, 126.1 us)
Async XLA Ops:
  7.2 239.9 %copy-start = (bf16[512,2048]{1,0:T(8,128)(2,1)S(1)}, bf16[512,2048]{1,0:T(8,128)(2,1)}, u32[]{:S(2)}) copy-start(bf16[512,2048]{1,0:T(8,128)(2,1)} %param.29) | copy-start | bytes 6291460
  7.2 6.8 %copy-start.10 = (s32[6,16,1]{1,2,0:T(1,128)S(1)}, s32[6,16,1]{1,2,0:T(1,128)}, u32[]{:S(2)}) copy-start(s32[6,16,1]{1,2,0:T(1,128)} %param.23) | copy-start | bytes 1156
  7.2 6.8 %copy-start.9 = (s32[6,16]{1,0:T(8,128)S(1)}, s32[6,16]{1,0:T(8,128)}, u32[]{:S(2)}) copy-start(s32[6,16]{1,0:T(8,128)} %param.24) | copy-start | bytes 1156
  7.2 6.8 %copy-start.12 = (s32[6]{0:T(128)S(1)}, s32[6]{0:T(128)}, u32[]{:S(2)}) copy-start(s32[6]{0:T(128)} %param.25) | copy-start | bytes 76
  7.2 6.9 %copy-start.8 = (f32[4,2048]{1,0:T(4,128)S(1)}, f32[4,2048]{1,0:T(4,128)}, u32[]{:S(2)}) copy-start(f32[4,2048]{1,0:T(4,128)} %param.20) | copy-start | bytes 98308
  7.2 132.9 %all-gather.3.cloned.1.call-start = ((), (), s32[]{:S(2)}) async-start(), calls=%async_computation.1 | async-start | bytes 21168128 | tf_op jit(solution)/shard_map/all_gather | solution.py:37
  8.0 237.6 %all-reduce.3.cloned.1.call-start = ((), (), s32[]{:S(2)}) async-start(), calls=%async_computation.4 | async-start | bytes 2523136 | tf_op jit(solution)/shard_map/psum | solution.py:60
  159.6 2.6 copy-start.3
  166.6 4.4 copy-start.11
  171.1 10.1 %copy-start.13 = (bf16[2048,512]{1,0:T(8,128)(2,1)S(1)}, bf16[2048,512]{1,0:T(8,128)(2,1)}, u32[]{:S(2)}) copy-start(bf16[2048,512]{1,0:T(8,128)(2,1)} %param.26) | copy-start | bytes 6291460
  181.1 2.4 copy-start.5
  183.6 2.3 copy-start.6
  185.0 268.1 %all-gather.5.cloned.1.call-start = ((), (), s32[]{:S(2)}) async-start(), calls=%async_computation.2 | async-start | bytes 17825792 | tf_op jit(solution)/shard_map/all_gather | solution.py:93
  185.8 320.9 %reduce-scatter.2.cloned.1.call-start = ((), (), s32[]{:S(2)}) async-start(), calls=%async_computation.3 | async-start | bytes 5308416 | tf_op jit(solution)/shard_map/reduce_scatter | solution.py:96
  193.7 53.4 %copy-start.14 = (f32[2048]{0:T(1024)S(1)}, f32[2048]{0:T(1024)}, u32[]{:S(2)}) copy-start(f32[2048]{0:T(1024)} %param.30) | copy-start | bytes 24580
  193.7 53.4 %copy-start.15 = (f32[512]{0:T(512)S(1)}, f32[512]{0:T(512)}, u32[]{:S(2)}) copy-start(f32[512]{0:T(512)} %param.28) | copy-start | bytes 6148
  251.9 5.5 %copy-start.7 = (f32[576,32]{0,1:T(8,128)S(1)}, f32[576,32]{0,1:T(8,128)}, u32[]{:S(2)}) copy-start(f32[576,32]{0,1:T(8,128)} %get-tuple-element.96) | copy-start | bytes 221188
  251.9 6.8 %copy-start.4 = (f32[2048]{0:T(1024)S(1)}, f32[2048]{0:T(1024)}, u32[]{:S(2)}) copy-start(f32[2048]{0:T(1024)} %param.32) | copy-start | bytes 24580
  444.8 8.3 %copy-start.2 = (f32[6,16,2048]{2,1,0:T(8,128)}, f32[6,16,2048]{2,1,0:T(8,128)S(1)}, u32[]{:S(2)}) copy-start(f32[6,16,2048]{2,1,0:T(8,128)S(1)} %get-tuple-element.49) | copy-start | bytes 2359300
  453.1 53.6 %copy-start.1 = (bf16[512,2048]{1,0:T(8,128)(2,1)S(1)}, bf16[512,2048]{1,0:T(8,128)(2,1)}, u32[]{:S(2)}) copy-start(bf16[512,2048]{1,0:T(8,128)(2,1)} %param.29) | copy-start | bytes 6291460
Sparse Core Ops, SparseCore 0:
  10.2 129.8 all-gather.2
  185.2 60.4 all-reduce.2
  247.7 120.2 all-gather.4
  469.0 37.6 reduce-scatter.1
where the time goes:
time: 523 us; the launch traced here: 513 us
  waiting for transfers between devices  213 us (41%)
  other arithmetic  180 us (34%)
  local copies, waits for them, and re-layouts  81.3 us (16%)
  matrix products  24.4 us (5%)
  between operations  14 us (3%)
    all_gather x1, waiting for transfers between devices, body(): row_block = lax.all_gather(state_pool, 'dp', axis=0, tiled=True)  126 us
    while x84, other arithmetic  72.6 us
    reduce_sum x36, other arithmetic, advance(): jnp.sum(c_now[:, :, None] * carried, axis=1) + skip_gain * signal_now  53 us
    psum x1, waiting for transfers between devices, body(): step_low, coupling = lax.psum((step_part, coupling_part), 'tensor')  47.5 us
    reduce_scatter x1, waiting for transfers between devices, body(): lax.psum_scatter(partials.astype(jnp.bfloat16), 'tensor', scatter_dimensi...  37.8 us
    gather x2, local copies, waits for them, and re-layouts, body(): jnp.take(row_block, jnp.clip(wanted, 0, row_block.shape[0] - 1), axis=0)  16.2 us
    mul x12, other arithmetic, advance(): step_now * signal_now  16 us
    dot_general x1, matrix products, body(): jnp.dot(gated_out, lax.all_gather(out_weight, 'dp', axis=1, tiled=True),...  15.8 us
  transfers between devices with their start and end apart: 4, of which 3 were waited for; matrix products, arithmetic and copies ran while one was open for 44% of the time, Pallas kernels for 0%

commit v1 on v0

v1 whole, which is shorter than its diff:
```python
import jax
import jax.numpy as jnp
from jax import lax
from jax.experimental import pallas as pl
from jax.experimental.pallas import tpu as pltpu
from jax.sharding import PartitionSpec as P

EPSILON = 1e-06
LOG2E = 1.4426950408889634
MESH = pl.DeviceIdType.MESH
F32 = jnp.float32
BF16 = jnp.bfloat16

SESS, NEW, ROWS = 6, 96, 576
CB, LANES, CH = 16, 128, 2048
NS, KW, RANK, ENT = 16, 4, 512, 19
PAGE = CH // CB * ENT
HALF = 10 * LANES
RB = 80
PW = RANK + LANES
QR = 1024


def gather_label(q, da, db, p):
    return ((q * 4 + da) * 4 + db) * 2 + p


def gather_events():
    groups = (
        [(0, 0)],
        [(1, 0), (3, 0)],
        [(0, 1), (0, 3), (2, 0)],
        [(1, 1), (1, 3), (3, 1), (3, 3)],
        [(0, 2)],
        [(2, 1), (2, 3)],
        [(1, 2), (3, 2)],
        [(2, 2)],
    )
    return [(q, da, db, p) for g in groups for (da, db) in g for p in (0, 1) for q in (0, 1)]


def gather_forwards(q, da, db, p):
    out = []
    if db == 0:
        if da == 0:
            out += [("a", 1, (q, 1, 0, p)), ("a", 3, (q, 3, 0, p))]
        if da == 1 and p == 0:
            out.append(("a", 1, (q, 2, 0, 0)))
        if da == 3 and p == 1:
            out.append(("a", 3, (q, 2, 0, 1)))
        out += [("b", 1, (q, da, 1, p)), ("b", 3, (q, da, 3, p))]
    else:
        if db == 1 and p == 0:
            out.append(("b", 1, (q, da, 2, 0)))
        if db == 3 and p == 1:
            out.append(("b", 3, (q, da, 2, 1)))
    return out


def sigmoid(v):
    return 0.5 * (1.0 + jnp.tanh(0.5 * v))


def dot_nt(a, b):
    return lax.dot_general(a, b, (((1,), (1,)), ((), ())), preferred_element_type=F32)


def dot(a, b):
    return jnp.dot(a, b, preferred_element_type=F32)


def iota(shape, dim):
    return lax.broadcasted_iota(jnp.int32, shape, dim)


def kernel(
    conv_w, conv_b, meta, coup_w, step_gain, step_b, decay_log, skip,
    conv_in, gate_in, pool, step_in_w, step_w, out_w,
    mixer_out, final_state,
    W, G, XN, GN, SIW, SWV, S2, D2, PL, PP, REQ, RQIN, PS, PRV, S8, P8, RALL, FT,
    SPB, CPW, RSS, RSR, AGB, EB, BC, FSB, FSV, OB, RBO, OUTV,
    loc_sem, ag_send, ag_recv, sib_send, sib_recv, rq_send, rq_recv,
    pa_send, pa_recv, pb_send, pb_recv, rs_send, rs_recv, an_send, an_recv,
    gx_send, gx_recv, ob_send, ob_recv, fs_sem,
):
    dp = lax.axis_index("dp")
    tn = lax.axis_index("tensor")
    x, z = dp // 4, dp % 4
    core = tn % 2
    sib = tn + 1 - 2 * core
    sends = []

    def remote(src, dst, ssem, rsem, to):
        c = pltpu.make_async_remote_copy(
            src_ref=src, dst_ref=dst, send_sem=ssem, recv_sem=rsem,
            device_id=to, device_id_type=MESH,
        )
        c.start()
        sends.append(c)

    def arrived(ref, ssem, rsem):
        pltpu.make_async_remote_copy(
            src_ref=ref, dst_ref=ref, send_sem=ssem, recv_sem=rsem,
            device_id=(dp, tn), device_id_type=MESH,
        ).wait_recv()

    def local(src, dst, k):
        c = pltpu.make_async_copy(src, dst, loc_sem.at[k])
        c.start()
        return c

    own_rows = pl.multiple_of(core * CH, CH)
    sib_rows = pl.multiple_of(CH - core * CH, CH)
    own_lanes = pl.multiple_of(core * LANES, LANES)
    sib_lanes = pl.multiple_of(LANES - core * LANES, LANES)
    ld_w = local(out_w.at[:, pl.ds(own_lanes, LANES)], W.at[dp, pl.ds(own_rows, CH)], 0)
    ld_pool = local(pool, PL, 1)
    ld_x = local(conv_in, XN, 2)
    ld_siw = local(step_in_w, SIW, 3)
    ld_sw = local(step_w, SWV, 4)
    ld_g = local(gate_in, GN, 5)

    bar = pltpu.get_barrier_semaphore()
    for d in range(1, 16):
        pl.semaphore_signal(bar, inc=1, device_id=((dp + d) % 16, tn), device_id_type=MESH)
    for d in range(1, 8):
        pl.semaphore_signal(bar, inc=1, device_id=(dp, (tn + d) % 8), device_id_type=MESH)
    pl.semaphore_wait(bar, 22)

    def part_rows(q, p):
        base = own_rows if q == 0 else sib_rows
        return pl.ds(pl.multiple_of(base + p * QR, QR), QR)

    def dp_of(q, a, b):
        return a * 4 + b if q == 0 else b * 4 + a

    def coords(q):
        return (x, z) if q == 0 else (z, x)

    def part(q, da, db, p):
        a, b = coords(q)
        return W.at[dp_of(q, (a + 4 - da) % 4, (b + 4 - db) % 4), part_rows(q, p)]

    def gather_step(label):
        q, da, db, p = label
        a, b = coords(q)
        ref = part(q, da, db, p)
        if (da, db) != (0, 0):
            k = gather_label(*label)
            arrived(ref, ag_send.at[k], ag_recv.at[k])
        elif q == 1:
            arrived(ref, sib_send.at[p], sib_recv.at[p])
        for axis, step, nlabel in gather_forwards(*label):
            k = gather_label(*nlabel)
            to = ((a + step) % 4, b) if axis == "a" else (a, (b + step) % 4)
            remote(ref, ref, ag_send.at[k], ag_recv.at[k], (dp_of(q, *to), tn))

    events = gather_events()
    cursor = [0]

    def advance(upto):
        while cursor[0] < min(upto, len(events)):
            gather_step(events[cursor[0]])
            cursor[0] += 1

    for p in (0, 1):
        remote(
            out_w.at[pl.ds(p * QR, QR), pl.ds(sib_lanes, LANES)],
            W.at[dp, part_rows(0, p)], sib_send.at[p], sib_recv.at[p], (dp, sib),
        )

    owner, slot, stored = meta[0:1, :], meta[1:2, :], meta[2:3, :]
    own_hot = (owner == iota((16, LANES), 0)).astype(F32)
    before = (iota((LANES, LANES), 0) < iota((LANES, LANES), 1)).astype(F32).astype(BF16)
    ahead = dot(own_hot.astype(BF16), before)
    rank = jnp.sum(own_hot * ahead, axis=0, keepdims=True).astype(jnp.int32)
    ask_row = jnp.where(stored > 0, owner * 16 + rank, -1)
    got_row = jnp.where(stored > 0, jnp.where(rank < 8, owner * 8 + rank, LANES + owner), -1)
    row_io = iota((256, LANES), 0)
    ask = (ask_row == row_io).astype(F32).astype(BF16)
    slot_hot = (iota((LANES, LANES), 0) == slot).astype(F32).astype(BF16)
    REQ[...] = dot_nt(ask, slot_hot).astype(BF16).reshape(16, 16, LANES)
    RQIN[dp] = REQ[dp]
    for d in range(1, 16):
        to = (dp + d) % 16
        remote(REQ.at[to], RQIN.at[dp], rq_send.at[d], rq_recv.at[d], (to, tn))
    got = (got_row == row_io).astype(F32).T[0:96, :].astype(BF16)

    ld_w.wait()
    advance(4)

    ld_pool.wait()
    pool_low = PL[...].astype(BF16)

    def permute(e, _):
        pick = (iota((PAGE, LANES), 0) - ENT * iota((PAGE, LANES), 1) == e).astype(F32)
        PP[:, pl.ds(pl.multiple_of(e * LANES, LANES), LANES)] = dot(
            pool_low, pick.astype(BF16)
        ).astype(BF16)
        return 0

    lax.fori_loop(0, ENT, permute, 0)
    PP[:, ENT * LANES :] = jnp.zeros((LANES, LANES), BF16)

    for d in range(1, 16):
        src = (dp + 16 - d) % 16
        arrived(RQIN.at[src], rq_send.at[d], rq_recv.at[d])
    asked = RQIN[...].astype(F32)
    first8 = asked[:, 0:8, :].reshape(LANES, LANES).astype(BF16)
    low = dot(first8, PP[:, 0:HALF]).reshape(16, 8, HALF)
    high = dot(first8, PP[:, HALF : 2 * HALF]).reshape(16, 8, HALF)
    PS[...] = jnp.concatenate([low, high], axis=1).astype(BF16)
    ninth = dot(asked[:, 8, :].astype(BF16), PP[...])
    S8[...] = ninth.reshape(16, 1, 2 * HALF)
    PRV[dp] = PS[dp]
    P8[dp] = S8[dp]
    for d in range(1, 16):
        to = (dp + d) % 16
        remote(PS.at[to], PRV.at[dp], pa_send.at[d], pa_recv.at[d], (to, tn))
        remote(S8.at[to], P8.at[dp], pb_send.at[d], pb_recv.at[d], (to, tn))

    for p in range(CB):
        cols = slice(p * LANES, (p + 1) * LANES)
        SPB[pl.ds(p, KW, stride=CB), :] = conv_w[:, cols]
        SPB[pl.ds(4 * CB + p, 1), :] = conv_b[:, cols]
        SPB[pl.ds(5 * CB + p, 1), :] = skip[:, cols]
        SPB[pl.ds(8 * CB + p, NS, stride=CB), :] = -LOG2E * jnp.exp(decay_log[:, cols])
    EB[...] = (iota((LANES, 2 * NS * LANES), 0) == iota((LANES, 2 * NS * LANES), 1) // LANES).astype(
        F32
    ).astype(BF16)
    CPW[...] = jnp.zeros_like(CPW)
    CPW[0 : 2 * NS, :] = coup_w[...]
    RSS[ROWS:, :] = jnp.zeros((8 * RB - ROWS, PW), BF16)

    ld_x.wait()

    def spread(g, _):
        r = pl.multiple_of(g * 16, 16)
        for p in range(CB):
            S2[pl.ds(g * 256 + p, 16, stride=CB), :] = XN[
                pl.ds(r, 16), p * LANES : (p + 1) * LANES
            ].astype(F32)
        return 0

    lax.fori_loop(0, ROWS // 16, spread, 0)

    for d in range(1, 16):
        src = (dp + 16 - d) % 16
        arrived(PRV.at[src], pa_send.at[d], pa_recv.at[d])
        arrived(P8.at[src], pb_send.at[d], pb_recv.at[d])

    for s in range(2):
        for o in range(16):
            RALL[o * 8 : o * 8 + 8, :] = PRV[o].astype(F32)[8 * s : 8 * s + 8, :]
        RALL[LANES : LANES + 16, :] = P8[...].reshape(16, 2 * HALF)[:, s * HALF : (s + 1) * HALF]
        RALL[LANES + 16 :, :] = jnp.zeros((LANES - 16, HALF), F32)
        FT[:, s * HALF : (s + 1) * HALF] = dot(got, RALL[...].astype(BF16))

    taps = [SPB[w * CB : (w + 1) * CB, :] for w in range(KW)]
    bias = SPB[4 * CB : 5 * CB, :]

    def conv_session(s, _):
        def old(w):
            return FT[
                pl.ds(pl.multiple_of(s * CB, CB), CB), (NS + w) * LANES : (NS + w + 1) * LANES
            ]

        def step(i, hist):
            h3, h2, h1 = hist
            for u in range(8):
                at = pl.ds(pl.multiple_of((s * NEW + i * 8 + u) * CB, CB), CB)
                now = S2[at, :]
                pre = bias + taps[0] * h3 + taps[1] * h2 + taps[2] * h1 + taps[3] * now
                S2[at, :] = pre * sigmoid(pre)
                h3, h2, h1 = h2, h1, now
            return (h3, h2, h1)

        lax.fori_loop(0, NEW // 8, step, (old(0), old(1), old(2)))
        return 0

    lax.fori_loop(0, SESS, conv_session, 0)

    def collect(g, _):
        r = pl.multiple_of(g * 16, 16)
        for p in range(CB):
            XN[pl.ds(r, 16), p * LANES : (p + 1) * LANES] = S2[
                pl.ds(g * 256 + p, 16, stride=CB), :
            ].astype(BF16)
        return 0

    lax.fori_loop(0, ROWS // 16, collect, 0)

    ld_siw.wait()

    def project(m, _):
        r = pl.ds(pl.multiple_of(m * 96, 96), 96)
        RSS[r, 0:RANK] = dot(XN[r, :], SIW[...]).astype(BF16)
        RSS[r, RANK:] = dot_nt(XN[r, :], CPW[...]).astype(BF16)
        return 0

    lax.fori_loop(0, ROWS // 96, project, 0)
    for d in range(1, 8):
        to = (tn + d) % 8
        remote(
            RSS.at[pl.ds(pl.multiple_of(to * RB, 16), RB)], RSR.at[d],
            rs_send.at[d], rs_recv.at[d], (dp, to),
        )
    advance(8)
    mine = pl.ds(pl.multiple_of(tn * RB, 16), RB)
    total = RSS[mine, :].astype(F32)
    for d in range(1, 8):
        arrived(RSR.at[d], rs_send.at[d], rs_recv.at[d])
        total = total + RSR[d].astype(F32)
    step_low = total[:, 0:RANK]
    inv_rms = lax.rsqrt(jnp.mean(step_low * step_low, axis=-1, keepdims=True) + EPSILON)
    AGB[mine, 0:RANK] = (step_low * inv_rms * step_gain[...]).astype(BF16)
    AGB[mine, RANK:] = total[:, RANK:].astype(BF16)
    for d in range(1, 8):
        to = (tn + d) % 8
        remote(AGB.at[mine], AGB.at[mine], an_send.at[d], an_recv.at[d], (dp, to))
    advance(16)
    for d in range(1, 8):
        src = (tn + 8 - d) % 8
        arrived(
            AGB.at[pl.ds(pl.multiple_of(src * RB, 16), RB)], an_send.at[d], an_recv.at[d]
        )

    ld_sw.wait()

    def step_size(m, _):
        r = pl.ds(pl.multiple_of(m * 96, 96), 96)
        for p in range(0, CB, 2):
            cols = slice(p * LANES, (p + 2) * LANES)
            v = dot(AGB[r, 0:RANK], SWV[:, cols]) + step_b[:, cols]
            v = jnp.maximum(v, 0.0) + jnp.log1p(jnp.exp(-jnp.abs(v)))
            for i in (0, 1):
                D2[pl.ds(m * 96 * CB + p + i, 96, stride=CB), :] = v[:, i * LANES : (i + 1) * LANES]
        return 0

    lax.fori_loop(0, ROWS // 96, step_size, 0)
    advance(20)

    ld_g.wait()
    outs = []
    for s in range(SESS):
        both = dot(AGB[s * NEW : (s + 1) * NEW, RANK:], EB[...])
        for n in range(2 * NS):
            BC[n * NEW : (n + 1) * NEW, :] = both[:, n * LANES : (n + 1) * LANES]
        for h in (0, 1):
            rate = [SPB[(8 + n) * CB + 8 * h : (8 + n) * CB + 8 * h + 8, :] for n in range(NS)]
            direct = SPB[5 * CB + 8 * h : 5 * CB + 8 * h + 8, :]
            start = tuple(
                FT[s * CB + 8 * h : s * CB + 8 * h + 8, n * LANES : (n + 1) * LANES]
                for n in range(NS)
            )

            def token(i, state, h=h, s=s, rate=rate, direct=direct):
                state = list(state)
                for u in range(4):
                    t = i * 4 + u
                    at = pl.ds(pl.multiple_of((s * NEW + t) * CB + 8 * h, 8), 8)
                    dt, sg = D2[at, :], S2[at, :]
                    dx = dt * sg
                    acc = [direct * sg, None]
                    for n in range(NS):
                        bn = BC[pl.ds(n * NEW + t, 8, stride=0), :]
                        cn = BC[pl.ds((NS + n) * NEW + t, 8, stride=0), :]
                        state[n] = jnp.exp2(dt * rate[n]) * state[n] + dx * bn
                        term = cn * state[n]
                        acc[n % 2] = term if acc[n % 2] is None else acc[n % 2] + term
                    S2[at, :] = acc[0] + acc[1]
                return tuple(state)

            last = lax.fori_loop(0, NEW // 4, token, start)
            for n in range(NS):
                FSB[n * CB + 8 * h : n * CB + 8 * h + 8, :] = last[n]
        for p in range(CB):
            FSV[s, :, p * LANES : (p + 1) * LANES] = FSB[pl.ds(p, NS, stride=CB), :]
        c = pltpu.make_async_copy(FSV.at[s], final_state.at[s], fs_sem.at[s])
        c.start()
        outs.append(c)

        def gate(g, _, s=s):
            r = pl.ds(pl.multiple_of(s * NEW + g * 16, 16), 16)
            for p in range(CB):
                cols = slice(p * LANES, (p + 1) * LANES)
                gt = GN[r, cols].astype(F32)
                y = S2[pl.ds((s * NEW + g * 16) * CB + p, 16, stride=CB), :]
                G[core, r, cols] = (y * (gt * sigmoid(gt))).astype(BF16)
            return 0

        lax.fori_loop(0, NEW // 16, gate, 0)
        here = G.at[core, pl.ds(s * NEW, NEW)]
        remote(here, here, gx_send.at[s], gx_recv.at[s], (dp, sib))
        advance(20 + 6 * (s + 1))

    for s in range(SESS):
        arrived(G.at[1 - core, pl.ds(s * NEW, NEW)], gx_send.at[s], gx_recv.at[s])

    def multiply(dx, dz):
        src = ((x + 4 - dx) % 4) * 4 + (z + 4 - dz) % 4
        to, side = src // 2, src % 2

        def rows(m, _):
            r = pl.ds(pl.multiple_of(m * 192, 192), 192)
            v = dot(G[0, r, :], W[src, 0:CH, :]) + dot(G[1, r, :], W[src, CH : 2 * CH, :])
            OB[src, r, :] = v.astype(BF16)
            return 0

        lax.fori_loop(0, ROWS // 192, rows, 0)

        @pl.when(to != tn)
        def _():
            c = pltpu.make_async_remote_copy(
                src_ref=OB.at[src], dst_ref=RBO.at[tn, side], send_sem=ob_send.at[src],
                recv_sem=ob_recv.at[tn, side], device_id=(dp, to), device_id_type=MESH,
            )
            c.start()

        @pl.when(to == tn)
        def _():
            RBO[tn, side] = OB[src]

    seen = {}
    for i, (q, da, db, p) in enumerate(events):
        key = (da, db) if q == 0 else (db, da)
        seen[key] = max(seen.get(key, 0), i)
    for key in sorted(seen, key=lambda k: seen[k]):
        advance(seen[key] + 1)
        multiply(*key)
    advance(len(events))

    for d in range(8):
        src = (tn + 8 - d) % 8
        for side in (0, 1):
            if d:
                arrived(RBO.at[src, side], ob_send.at[0], ob_recv.at[src, side])
    for c in (0, 1):
        for side in (0, 1):
            cols = slice(side * 256 + c * LANES, side * 256 + (c + 1) * LANES)

            def finish(m, _, c=c, side=side, cols=cols):
                r = pl.ds(pl.multiple_of(m * 96, 96), 96)
                v = RBO[c, side, r, :].astype(F32)
                for y in range(1, 4):
                    v = v + RBO[2 * y + c, side, r, :].astype(F32)
                OUTV[r, cols] = v.astype(BF16)
                return 0

            lax.fori_loop(0, ROWS // 96, finish, 0)
    c = pltpu.make_async_copy(OUTV, mixer_out, fs_sem.at[SESS])
    c.start()
    outs.append(c)
    for src in range(16):

        @pl.when(src // 2 != tn)
        def _(src=src):
            pltpu.make_async_remote_copy(
                src_ref=OB.at[src], dst_ref=OB.at[src], send_sem=ob_send.at[src],
                recv_sem=ob_recv.at[0, 0], device_id=(dp, tn), device_id_type=MESH,
            ).wait_send()

    for c in sends:
        c.wait_send()
    for c in outs:
        c.wait()


def body(
    conv_input, gate_input, conv_weight, conv_bias, state_pool, page_owner, page_slot, page_count,
    step_in_weight, coupling_weight, step_gain, step_weight, step_bias, decay_log, skip_gain,
    out_weight,
):
    pages = page_slot.shape[1]
    stored = jnp.arange(pages, dtype=jnp.int32)[None, :] < page_count[:, None]
    rows = jnp.stack(
        [page_owner[:, :, 0].reshape(-1), page_slot.reshape(-1), stored.astype(jnp.int32).reshape(-1)]
    )
    meta = jnp.pad(rows, ((0, 5), (0, LANES - rows.shape[1])), constant_values=-1)
    vmem = pl.BlockSpec(memory_space=pltpu.VMEM)
    hbm = pl.BlockSpec(memory_space=pl.ANY)
    sem = pltpu.SemaphoreType.DMA
    mixer_out, final_state = pl.pallas_call(
        kernel,
        out_shape=(
            jax.ShapeDtypeStruct((ROWS, 512), BF16),
            jax.ShapeDtypeStruct((SESS, NS, CH), F32),
        ),
        in_specs=[vmem] * 8 + [hbm] * 6,
        out_specs=(hbm, hbm),
        scratch_shapes=[
            pltpu.VMEM((16, 2 * CH, LANES), BF16),
            pltpu.VMEM((2, ROWS, CH), BF16),
            pltpu.VMEM((ROWS, CH), BF16),
            pltpu.VMEM((ROWS, CH), BF16),
            pltpu.VMEM((CH, RANK), BF16),
            pltpu.VMEM((RANK, CH), BF16),
            pltpu.VMEM((ROWS * CB, LANES), F32),
            pltpu.VMEM((ROWS * CB, LANES), F32),
            pltpu.VMEM((LANES, PAGE), F32),
            pltpu.VMEM((LANES, 2 * HALF), BF16),
            pltpu.VMEM((16, 16, LANES), BF16),
            pltpu.VMEM((16, 16, LANES), BF16),
            pltpu.VMEM((16, 16, HALF), BF16),
            pltpu.VMEM((16, 16, HALF), BF16),
            pltpu.VMEM((16, 1, 2 * HALF), F32),
            pltpu.VMEM((16, 1, 2 * HALF), F32),
            pltpu.VMEM((256, HALF), F32),
            pltpu.VMEM((96, 2 * HALF), F32),
            pltpu.VMEM((24 * CB, LANES), F32),
            pltpu.VMEM((LANES, CH), BF16),
            pltpu.VMEM((8 * RB, PW), BF16),
            pltpu.VMEM((8, RB, PW), BF16),
            pltpu.VMEM((8 * RB, PW), BF16),
            pltpu.VMEM((LANES, 2 * NS * LANES), BF16),
            pltpu.VMEM((2 * NS * NEW, LANES), F32),
            pltpu.VMEM((NS * CB, LANES), F32),
            pltpu.VMEM((SESS, NS, CH), F32),
            pltpu.VMEM((16, ROWS, LANES), BF16),
            pltpu.VMEM((8, 2, ROWS, LANES), BF16),
            pltpu.VMEM((ROWS, 512), BF16),
            sem((6,)), sem((64,)), sem((64,)), sem((2,)), sem((2,)), sem((16,)), sem((16,)),
            sem((16,)), sem((16,)), sem((16,)), sem((16,)), sem((8,)), sem((8,)), sem((8,)), sem((8,)),
            sem((SESS,)), sem((SESS,)), sem((16,)), sem((8, 2)), sem((SESS + 1,)),
        ],
        compiler_params=pltpu.CompilerParams(
            collective_id=0, has_side_effects=True, vmem_limit_bytes=62 << 20
        ),
        cost_estimate=pl.CostEstimate(
            flops=2 * ROWS * CH * (4096 + 1056), bytes_accessed=12 << 20, transcendentals=20 << 20
        ),
    )(
        conv_weight, conv_bias.reshape(1, -1), meta, coupling_weight, step_gain.reshape(1, -1),
        step_bias.reshape(1, -1), decay_log, skip_gain.reshape(1, -1),
        conv_input.reshape(ROWS, CH), gate_input.reshape(ROWS, CH), state_pool,
        step_in_weight, step_weight, out_weight,
    )
    return mixer_out.reshape(SESS, NEW, 512), final_state


def solution(mesh):
    return jax.shard_map(
        body,
        mesh=mesh,
        in_specs=(
            P("dp", None, "tensor"),
            P("dp", None, "tensor"),
            P(None, "tensor"),
            P("tensor"),
            P("dp", "tensor"),
            P("dp", None, None),
            P("dp", None),
            P("dp"),
            P("tensor", None),
            P(None, "tensor"),
            P(),
            P(None, "tensor"),
            P("tensor"),
            P(None, "tensor"),
            P("tensor"),
            P("tensor", "dp"),
        ),
        out_specs=(P("dp", None, "tensor"), P("dp", None, "tensor")),
        check_vma=False,
    )
```

time: 523 us -> 166 us (0.32); the launches traced: 513 us -> 165 us
  waiting for transfers between devices: 213 us -> 0 us
  other arithmetic: 180 us -> 1.44 us
  Pallas kernels: 0 us -> 158 us
  local copies, waits for them, and re-layouts: 81.3 us -> 5.53 us
  matrix products: 24.4 us -> 0 us
  between operations: 14 us -> 0.64 us
    pallas_call x0 -> x1, Pallas kernels: none -> 158 us  [body(): pl.pallas_call(kernel, out_shape=(jax.ShapeDtypeStruct((ROWS, 512), BF16)...]
    all_gather x2 -> x0, waiting for transfers between devices: 126 us -> none  [the longest x1 126 us: body(): row_block = lax.all_gather(state_pool, 'dp', axis=0, tiled=True)]
    while x84 -> x0, other arithmetic: 72.6 us -> none
    reduce_sum x37 -> x0, other arithmetic: 54.4 us -> none  [the longest x36 53 us: advance(): jnp.sum(c_now[:, :, None] * carried, axis=1) + skip_gain * signal_now]
    psum x1 -> x0, waiting for transfers between devices: 47.5 us -> none  [body(): step_low, coupling = lax.psum((step_part, coupling_part), 'tensor')]
    reduce_scatter x1 -> x0, waiting for transfers between devices: 37.8 us -> none  [body(): lax.psum_scatter(partials.astype(jnp.bfloat16), 'tensor', scatter_dimensi...]
    dot_general x4 -> x0, matrix products: 24.4 us -> none  [the longest x1 15.8 us: body(): jnp.dot(gated_out, lax.all_gather(out_weight, 'dp', axis=1, tiled=True),...]
    mul x25 -> x0, local copies, waits for them, and re-layouts: 23.7 us -> none  [the longest x12 13.5 us: advance(): step_now[:, None, :] * decay_rate[None]]
  transfers between devices with their start and end apart: 4 -> 0, of which waited for: 3 -> 0; matrix products, arithmetic and copies ran while one was open for 44% -> 0% of each run, Pallas kernels for 0% -> 0%
where the time goes in v1:
time: 166 us; the launch traced here: 165 us
  Pallas kernels  158 us (95%)
  local copies, waits for them, and re-layouts  5.53 us (3%)
    pallas_call x1, Pallas kernels, body(): pl.pallas_call(kernel, out_shape=(jax.ShapeDtypeStruct((ROWS, 512), BF16)...  158 us
    unnamed x2, local copies, waits for them, and re-layouts  4 us

profile of v1, /device:TPU:5, one launch (start us, length us, event | category | flops | bytes accessed | tf_op | source)
XLA Modules:
  0.0 165.4 jit_solution(3232435081390181579)
XLA Ops:
  0.6 0.8 stack_reshape.4
  1.4 0.7 reduce
  2.1 0.1 stack_reshape_squeeze.3
  2.2 0.7 fusion
  2.9 0.1 reshape.60
  3.0 0.6 pad.4.meta
  3.6 157.8 %shard_map.167 = (bf16[576,512]{1,0:T(8,128)(2,1)}, f32[6,16,2048]{2,1,0:T(8,128)}) custom-call(f32[4,2048]{1,0:T(4,128)} %conv_w.1, f32[1,2048]{1,0:T(1,128)} %bitcast.10, s32[8,128]{1,0:T(8,128)} %pad.4.meta, bf16[32,2048]{1,0:T(8,128)(2,1)} %coup_w.1, f32[1,512]{1,0:T(1,128)} %bitcast.13, f32[1,2048]{1,0:T(1,128)} %bitcast.11, f32[16,2048]{1,0:T(8,128)} %decay_log.1, ...), custom_call_target="tpu_custom_call" | custom-call | flops 12155092992 | bytes 12582912 | tf_op jit(solution)/shard_map/pallas_call | solution.py:483
  161.4 1.9 %copy.20 = bf16[6,96,512]{2,1,0:T(8,128)(2,1)} copy(bf16[6,96,512]{2,1,0:T(8,128)(2,1)} %bitcast.7) | data formatting | bytes 1179648
  163.3 2.1 %copy.21 = f32[6,16,2048]{2,1,0:T(8,128)} copy(f32[6,16,2048]{2,1,0:T(8,128)} %get-tuple-element.9) | data formatting | bytes 1572864
  (1 shorter events, 0.0 us)

commit v2 on v1

--- a/solution.py
+++ b/solution.py
@@ -18,6 +18,7 @@
 HALF = 10 * LANES
 RB = 80
 PW = RANK + LANES
+FIX = 32
 QR = 1024
 
 
@@ -26,17 +27,32 @@
 
 
 def gather_events():
-    groups = (
-        [(0, 0)],
-        [(1, 0), (3, 0)],
-        [(0, 1), (0, 3), (2, 0)],
-        [(1, 1), (1, 3), (3, 1), (3, 3)],
-        [(0, 2)],
-        [(2, 1), (2, 3)],
-        [(1, 2), (3, 2)],
-        [(2, 2)],
-    )
-    return [(q, da, db, p) for g in groups for (da, db) in g for p in (0, 1) for q in (0, 1)]
+    return [
+        (0, 0, 0, 0), (0, 0, 0, 1), (1, 0, 0, 0), (1, 0, 0, 1),
+        (0, 0, 1, 0), (0, 0, 3, 0), (0, 1, 0, 0), (0, 3, 0, 0),
+        (0, 0, 3, 1), (0, 0, 1, 1), (0, 1, 0, 1), (0, 3, 0, 1),
+        (1, 1, 0, 0), (1, 0, 3, 0), (1, 0, 1, 0), (1, 3, 0, 0),
+        (1, 0, 3, 1), (1, 0, 1, 1), (1, 3, 0, 1), (1, 1, 0, 1),
+        (0, 1, 3, 0), (0, 2, 0, 0), (0, 2, 0, 1), (0, 0, 2, 0),
+        (0, 1, 1, 0), (0, 3, 3, 0), (1, 1, 3, 0), (1, 1, 1, 0),
+        (0, 3, 1, 0), (1, 3, 3, 0), (1, 0, 2, 0), (0, 0, 2, 1),
+        (1, 3, 1, 0), (0, 1, 1, 1), (0, 1, 3, 1), (1, 0, 2, 1),
+        (1, 3, 1, 1), (1, 3, 3, 1), (0, 3, 1, 1), (0, 3, 3, 1),
+        (1, 1, 1, 1), (1, 1, 3, 1), (1, 2, 0, 1), (1, 2, 0, 0),
+        (0, 2, 1, 0), (0, 2, 3, 0), (1, 1, 2, 0), (1, 3, 2, 1),
+        (0, 2, 1, 1), (0, 2, 3, 1), (1, 3, 2, 0), (1, 1, 2, 1),
+        (1, 2, 3, 1), (1, 2, 1, 1), (0, 1, 2, 1), (0, 1, 2, 0),
+        (1, 2, 1, 0), (1, 2, 3, 0), (0, 3, 2, 1), (0, 3, 2, 0),
+        (0, 2, 2, 0), (0, 2, 2, 1), (1, 2, 2, 1), (1, 2, 2, 0),
+    ]
+
+
+PAIRS = (
+    ((0, 0), (0, 1)), ((0, 3), (1, 0)), ((3, 0), (2, 0)), ((1, 3), (3, 3)),
+    ((1, 1), (3, 1)), ((0, 2), (2, 1)), ((2, 3), (1, 2)), ((3, 2), (2, 2)),
+)
+EARLY = 2
+HROWS = ROWS // 2
 
 
 def gather_forwards(q, da, db, p):
@@ -74,14 +90,15 @@
 
 
 def kernel(
-    conv_w, conv_b, meta, coup_w, step_gain, step_b, decay_log, skip,
+    page_owner, page_slot, page_count, conv_w, conv_b, coup_w, step_gain, step_b, decay_log, skip,
     conv_in, gate_in, pool, step_in_w, step_w, out_w,
     mixer_out, final_state,
     W, G, XN, GN, SIW, SWV, S2, D2, PL, PP, REQ, RQIN, PS, PRV, S8, P8, RALL, FT,
+    PRE, F2, XF, FXS, FXR,
     SPB, CPW, RSS, RSR, AGB, EB, BC, FSB, FSV, OB, RBO, OUTV,
     loc_sem, ag_send, ag_recv, sib_send, sib_recv, rq_send, rq_recv,
-    pa_send, pa_recv, pb_send, pb_recv, rs_send, rs_recv, an_send, an_recv,
-    gx_send, gx_recv, ob_send, ob_recv, fs_sem,
+    pa_send, pa_recv, pb_send, pb_recv, rs_send, rs_recv, an_send, an_recv, fx_send, fx_recv,
+    gx_send, gx_recv, ob_send, ob_recv, fs_sem, out_sem,
 ):
     dp = lax.axis_index("dp")
     tn = lax.axis_index("tensor")
@@ -90,13 +107,13 @@
     sib = tn + 1 - 2 * core
     sends = []
 
-    def remote(src, dst, ssem, rsem, to):
+    def remote(src, dst, ssem, rsem, to, kept=sends):
         c = pltpu.make_async_remote_copy(
             src_ref=src, dst_ref=dst, send_sem=ssem, recv_sem=rsem,
             device_id=to, device_id_type=MESH,
         )
         c.start()
-        sends.append(c)
+        kept.append(c)
 
     def arrived(ref, ssem, rsem):
         pltpu.make_async_remote_copy(
@@ -169,7 +186,23 @@
             W.at[dp, part_rows(0, p)], sib_send.at[p], sib_recv.at[p], (dp, sib),
         )
 
-    owner, slot, stored = meta[0:1, :], meta[1:2, :], meta[2:3, :]
+    row16 = iota((16, LANES), 0)
+    lane16 = iota((16, LANES), 1)
+    owner = jnp.zeros((16, LANES), jnp.int32)
+    spread16 = (lane16 % 16 == row16).astype(F32).astype(BF16)
+    slot = dot(page_slot[...].astype(F32).astype(BF16), spread16)
+    slot = jnp.where(iota((SESS, LANES), 0) == iota((SESS, LANES), 1) // 16, slot, 0.0)
+    slot = jnp.sum(slot, axis=0, keepdims=True).astype(jnp.int32)
+    for s in range(SESS):
+        here = lane16 == s * 16 + row16
+        owner = jnp.where(here, page_owner[s], owner)
+    lane = iota((1, LANES), 1)
+    owner = jnp.sum(owner.astype(F32), axis=0, keepdims=True).astype(jnp.int32)
+    owner = jnp.where(lane < 96, owner, 16)
+    count = jnp.zeros((1, LANES), jnp.int32)
+    for s in range(SESS):
+        count = jnp.where(lane // 16 == s, page_count[s], count)
+    stored = (lane % 16 < count).astype(jnp.int32)
     own_hot = (owner == iota((16, LANES), 0)).astype(F32)
     before = (iota((LANES, LANES), 0) < iota((LANES, LANES), 1)).astype(F32).astype(BF16)
     ahead = dot(own_hot.astype(BF16), before)
@@ -187,7 +220,7 @@
     got = (got_row == row_io).astype(F32).T[0:96, :].astype(BF16)
 
     ld_w.wait()
-    advance(4)
+    advance(1)
 
     ld_pool.wait()
     pool_low = PL[...].astype(BF16)
@@ -219,15 +252,14 @@
         remote(PS.at[to], PRV.at[dp], pa_send.at[d], pa_recv.at[d], (to, tn))
         remote(S8.at[to], P8.at[dp], pb_send.at[d], pb_recv.at[d], (to, tn))
 
+    advance(4)
+
     for p in range(CB):
         cols = slice(p * LANES, (p + 1) * LANES)
         SPB[pl.ds(p, KW, stride=CB), :] = conv_w[:, cols]
         SPB[pl.ds(4 * CB + p, 1), :] = conv_b[:, cols]
         SPB[pl.ds(5 * CB + p, 1), :] = skip[:, cols]
         SPB[pl.ds(8 * CB + p, NS, stride=CB), :] = -LOG2E * jnp.exp(decay_log[:, cols])
-    EB[...] = (iota((LANES, 2 * NS * LANES), 0) == iota((LANES, 2 * NS * LANES), 1) // LANES).astype(
-        F32
-    ).astype(BF16)
     CPW[...] = jnp.zeros_like(CPW)
     CPW[0 : 2 * NS, :] = coup_w[...]
     RSS[ROWS:, :] = jnp.zeros((8 * RB - ROWS, PW), BF16)
@@ -244,27 +276,18 @@
 
     lax.fori_loop(0, ROWS // 16, spread, 0)
 
-    for d in range(1, 16):
-        src = (dp + 16 - d) % 16
-        arrived(PRV.at[src], pa_send.at[d], pa_recv.at[d])
-        arrived(P8.at[src], pb_send.at[d], pb_recv.at[d])
-
-    for s in range(2):
-        for o in range(16):
-            RALL[o * 8 : o * 8 + 8, :] = PRV[o].astype(F32)[8 * s : 8 * s + 8, :]
-        RALL[LANES : LANES + 16, :] = P8[...].reshape(16, 2 * HALF)[:, s * HALF : (s + 1) * HALF]
-        RALL[LANES + 16 :, :] = jnp.zeros((LANES - 16, HALF), F32)
-        FT[:, s * HALF : (s + 1) * HALF] = dot(got, RALL[...].astype(BF16))
-
     taps = [SPB[w * CB : (w + 1) * CB, :] for w in range(KW)]
     bias = SPB[4 * CB : 5 * CB, :]
+    none = jnp.zeros((CB, LANES), F32)
+    for s in range(SESS):
+        raw = [S2[(s * NEW + t) * CB : (s * NEW + t + 1) * CB, :] for t in range(3)]
+        for t in range(3):
+            pre = bias
+            for u in range(t + 1):
+                pre = pre + taps[3 - t + u] * raw[u]
+            PRE[(s * 3 + t) * CB : (s * 3 + t + 1) * CB, :] = pre
 
     def conv_session(s, _):
-        def old(w):
-            return FT[
-                pl.ds(pl.multiple_of(s * CB, CB), CB), (NS + w) * LANES : (NS + w + 1) * LANES
-            ]
-
         def step(i, hist):
             h3, h2, h1 = hist
             for u in range(8):
@@ -275,7 +298,7 @@
                 h3, h2, h1 = h2, h1, now
             return (h3, h2, h1)
 
-        lax.fori_loop(0, NEW // 8, step, (old(0), old(1), old(2)))
+        lax.fori_loop(0, NEW // 8, step, (none, none, none))
         return 0
 
     lax.fori_loop(0, SESS, conv_session, 0)
@@ -306,24 +329,89 @@
             rs_send.at[d], rs_recv.at[d], (dp, to),
         )
     advance(8)
+
+    EB[...] = (iota((LANES, 2 * NS * LANES), 0) == iota((LANES, 2 * NS * LANES), 1) // LANES).astype(
+        F32
+    ).astype(BF16)
+    advance(8)
+
+    for d in range(1, 16):
+        src = (dp + 16 - d) % 16
+        arrived(PRV.at[src], pa_send.at[d], pa_recv.at[d])
+        arrived(P8.at[src], pb_send.at[d], pb_recv.at[d])
+
+    for s in range(2):
+        for o in range(16):
+            RALL[o * 8 : o * 8 + 8, :] = PRV[o].astype(F32)[8 * s : 8 * s + 8, :]
+        RALL[LANES : LANES + 16, :] = P8[...].reshape(16, 2 * HALF)[:, s * HALF : (s + 1) * HALF]
+        RALL[LANES + 16 :, :] = jnp.zeros((LANES - 16, HALF), F32)
+        FT[:, s * HALF : (s + 1) * HALF] = dot(got, RALL[...].astype(BF16))
+
+
+    advance(8)
+
+    F2[SESS * 3 * CB :, :] = jnp.zeros(((FIX - SESS * 3) * CB, LANES), F32)
+    for s in range(SESS):
+        hist = [
+            FT[s * CB : (s + 1) * CB, (NS + w) * LANES : (NS + w + 1) * LANES] for w in range(3)
+        ]
+        for t in range(3):
+            r = s * 3 + t
+            pre = PRE[r * CB : (r + 1) * CB, :]
+            for w in range(3 - t):
+                pre = pre + taps[w] * hist[t + w]
+            sg = pre * sigmoid(pre)
+            S2[(s * NEW + t) * CB : (s * NEW + t + 1) * CB, :] = sg
+            F2[r * CB : (r + 1) * CB, :] = sg
+    for p in range(CB):
+        XF[:, p * LANES : (p + 1) * LANES] = F2[pl.ds(p, FIX, stride=CB), :].astype(BF16)
+    FXS[:, 0:RANK] = dot(XF[...], SIW[...]).astype(BF16)
+    FXS[:, RANK:] = dot_nt(XF[...], CPW[...]).astype(BF16)
+    for d in range(1, 8):
+        to = (tn + d) % 8
+        remote(FXS, FXR.at[d], fx_send.at[d], fx_recv.at[d], (dp, to))
+
+    advance(8)
+
+    def normalize(sums):
+        low = sums[:, 0:RANK]
+        inv_rms = lax.rsqrt(jnp.mean(low * low, axis=-1, keepdims=True) + EPSILON)
+        return (low * inv_rms * step_gain[...]).astype(BF16), sums[:, RANK:].astype(BF16)
+
     mine = pl.ds(pl.multiple_of(tn * RB, 16), RB)
     total = RSS[mine, :].astype(F32)
     for d in range(1, 8):
         arrived(RSR.at[d], rs_send.at[d], rs_recv.at[d])
         total = total + RSR[d].astype(F32)
-    step_low = total[:, 0:RANK]
-    inv_rms = lax.rsqrt(jnp.mean(step_low * step_low, axis=-1, keepdims=True) + EPSILON)
-    AGB[mine, 0:RANK] = (step_low * inv_rms * step_gain[...]).astype(BF16)
-    AGB[mine, RANK:] = total[:, RANK:].astype(BF16)
+    AGB[mine, 0:RANK], AGB[mine, RANK:] = normalize(total)
+    an_sends = []
     for d in range(1, 8):
         to = (tn + d) % 8
-        remote(AGB.at[mine], AGB.at[mine], an_send.at[d], an_recv.at[d], (dp, to))
-    advance(16)
+        remote(AGB.at[mine], AGB.at[mine], an_send.at[d], an_recv.at[d], (dp, to), an_sends)
+    advance(12)
     for d in range(1, 8):
         src = (tn + 8 - d) % 8
         arrived(
             AGB.at[pl.ds(pl.multiple_of(src * RB, 16), RB)], an_send.at[d], an_recv.at[d]
         )
+
+    fixed = FXS[...].astype(F32)
+    for d in range(1, 8):
+        arrived(FXR.at[d], fx_send.at[d], fx_recv.at[d])
+        fixed = fixed + FXR[d].astype(F32)
+    normed, coupled = normalize(fixed)
+    place = iota((96, FIX), 0)
+    place = ((place % 16 < 3) & (place // 16 * 3 + place % 16 == iota((96, FIX), 1))).astype(F32)
+    placed = dot(place.astype(BF16), jnp.concatenate([normed, coupled], axis=1))
+    for c in an_sends:
+        c.wait_send()
+    for s in range(SESS):
+        r = slice(s * NEW, s * NEW + 16)
+        AGB[r, :] = jnp.where(
+            iota((16, PW), 0) < 3, placed[s * 16 : s * 16 + 16, :], AGB[r, :].astype(F32)
+        ).astype(BF16)
+
+    advance(16)
 
     ld_sw.wait()
 
@@ -339,6 +427,41 @@
 
     lax.fori_loop(0, ROWS // 96, step_size, 0)
     advance(20)
+
+    def gates(first, last):
+        for s in range(first, last):
+            arrived(G.at[1 - core, pl.ds(s * NEW, NEW)], gx_send.at[s], gx_recv.at[s])
+
+    last_event = {}
+    for i, (q, da, db, p) in enumerate(events):
+        last_event[(da, db) if q == 0 else (db, da)] = i
+
+    def multiply(pair, halves):
+        advance(max(last_event[key] for key in pair) + 1)
+        blocks = [((x + 4 - dx) % 4) * 4 + (z + 4 - dz) % 4 for dx, dz in pair]
+        r = slice(halves[0] * HROWS, (halves[-1] + 1) * HROWS)
+
+        def weight(k):
+            return jnp.concatenate([W[b, k * CH : (k + 1) * CH, :] for b in blocks], axis=1)
+
+        v = dot(G[0, r, :], weight(0)) + dot(G[1, r, :], weight(1))
+        for i, b in enumerate(blocks):
+            to, side = b // 2, b % 2
+            OB[b, r, :] = v[:, i * LANES : (i + 1) * LANES].astype(BF16)
+
+            @pl.when(to != tn)
+            def _(b=b, to=to, side=side):
+                for g in halves:
+                    rg = pl.ds(g * HROWS, HROWS)
+                    pltpu.make_async_remote_copy(
+                        src_ref=OB.at[b, rg], dst_ref=RBO.at[tn, side, rg],
+                        send_sem=ob_send.at[b, g], recv_sem=ob_recv.at[tn, side, g],
+                        device_id=(dp, to), device_id_type=MESH,
+                    ).start()
+
+            @pl.when(to == tn)
+            def _(b=b, side=side, r=r):
+                RBO[tn, side, r, :] = OB[b, r, :]
 
     ld_g.wait()
     outs = []
@@ -372,6 +495,7 @@
                 return tuple(state)
 
             last = lax.fori_loop(0, NEW // 4, token, start)
+            advance(20 + (5 * (2 * s + h + 1)) // 3)
             for n in range(NS):
                 FSB[n * CB + 8 * h : n * CB + 8 * h + 8, :] = last[n]
         for p in range(CB):
@@ -392,73 +516,50 @@
         lax.fori_loop(0, NEW // 16, gate, 0)
         here = G.at[core, pl.ds(s * NEW, NEW)]
         remote(here, here, gx_send.at[s], gx_recv.at[s], (dp, sib))
-        advance(20 + 6 * (s + 1))
-
-    for s in range(SESS):
-        arrived(G.at[1 - core, pl.ds(s * NEW, NEW)], gx_send.at[s], gx_recv.at[s])
-
-    def multiply(dx, dz):
-        src = ((x + 4 - dx) % 4) * 4 + (z + 4 - dz) % 4
-        to, side = src // 2, src % 2
-
-        def rows(m, _):
-            r = pl.ds(pl.multiple_of(m * 192, 192), 192)
-            v = dot(G[0, r, :], W[src, 0:CH, :]) + dot(G[1, r, :], W[src, CH : 2 * CH, :])
-            OB[src, r, :] = v.astype(BF16)
-            return 0
-
-        lax.fori_loop(0, ROWS // 192, rows, 0)
-
-        @pl.when(to != tn)
-        def _():
-            c = pltpu.make_async_remote_copy(
-                src_ref=OB.at[src], dst_ref=RBO.at[tn, side], send_sem=ob_send.at[src],
-                recv_sem=ob_recv.at[tn, side], device_id=(dp, to), device_id_type=MESH,
+        if s == SESS // 2 - 1:
+            gates(0, s + 1)
+            for pair in PAIRS[:EARLY]:
+                multiply(pair, (0,))
+
+    gates(SESS // 2, SESS)
+    for k, pair in enumerate(PAIRS):
+        multiply(pair, (1,) if k < EARLY else (0, 1))
+    advance(len(events))
+
+    for side in (1 - z % 2, z % 2):
+        for g in (0, 1):
+            rg = pl.ds(g * HROWS, HROWS)
+            for d in range(1, 8):
+                src = (tn + 8 - d) % 8
+                arrived(RBO.at[src, side, rg], ob_send.at[0, g], ob_recv.at[src, side, g])
+            for c in (0, 1):
+
+                def finish(m, _, c=c, g=g, side=side):
+                    r = pl.ds(pl.multiple_of(g * HROWS + m * 96, 32), 96)
+                    v = RBO[c, side, r, :].astype(F32)
+                    for y in range(1, 4):
+                        v = v + RBO[2 * y + c, side, r, :].astype(F32)
+                    at = pl.multiple_of(side * 256 + c * LANES, LANES)
+                    OUTV[r, pl.ds(at, LANES)] = v.astype(BF16)
+                    return 0
+
+                lax.fori_loop(0, HROWS // 96, finish, 0)
+            cols = pl.ds(pl.multiple_of(side * 256, 256), 256)
+            c = pltpu.make_async_copy(
+                OUTV.at[rg, cols], mixer_out.at[rg, cols], out_sem.at[side, g]
             )
             c.start()
-
-        @pl.when(to == tn)
-        def _():
-            RBO[tn, side] = OB[src]
-
-    seen = {}
-    for i, (q, da, db, p) in enumerate(events):
-        key = (da, db) if q == 0 else (db, da)
-        seen[key] = max(seen.get(key, 0), i)
-    for key in sorted(seen, key=lambda k: seen[k]):
-        advance(seen[key] + 1)
-        multiply(*key)
-    advance(len(events))
-
-    for d in range(8):
-        src = (tn + 8 - d) % 8
-        for side in (0, 1):
-            if d:
-                arrived(RBO.at[src, side], ob_send.at[0], ob_recv.at[src, side])
-    for c in (0, 1):
-        for side in (0, 1):
-            cols = slice(side * 256 + c * LANES, side * 256 + (c + 1) * LANES)
-
-            def finish(m, _, c=c, side=side, cols=cols):
-                r = pl.ds(pl.multiple_of(m * 96, 96), 96)
-                v = RBO[c, side, r, :].astype(F32)
-                for y in range(1, 4):
-                    v = v + RBO[2 * y + c, side, r, :].astype(F32)
-                OUTV[r, cols] = v.astype(BF16)
-                return 0
-
-            lax.fori_loop(0, ROWS // 96, finish, 0)
-    c = pltpu.make_async_copy(OUTV, mixer_out, fs_sem.at[SESS])
-    c.start()
-    outs.append(c)
+            outs.append(c)
     for src in range(16):
 
         @pl.when(src // 2 != tn)
         def _(src=src):
-            pltpu.make_async_remote_copy(
-                src_ref=OB.at[src], dst_ref=OB.at[src], send_sem=ob_send.at[src],
-                recv_sem=ob_recv.at[0, 0], device_id=(dp, tn), device_id_type=MESH,
-            ).wait_send()
+            for g in (0, 1):
+                ref = OB.at[src, pl.ds(g * HROWS, HROWS)]
+                pltpu.make_async_remote_copy(
+                    src_ref=ref, dst_ref=ref, send_sem=ob_send.at[src, g],
+                    recv_sem=ob_recv.at[0, 0, 0], device_id=(dp, tn), device_id_type=MESH,
+                ).wait_send()
 
     for c in sends:
         c.wait_send()
@@ -471,12 +572,6 @@
     step_in_weight, coupling_weight, step_gain, step_weight, step_bias, decay_log, skip_gain,
     out_weight,
 ):
-    pages = page_slot.shape[1]
-    stored = jnp.arange(pages, dtype=jnp.int32)[None, :] < page_count[:, None]
-    rows = jnp.stack(
-        [page_owner[:, :, 0].reshape(-1), page_slot.reshape(-1), stored.astype(jnp.int32).reshape(-1)]
-    )
-    meta = jnp.pad(rows, ((0, 5), (0, LANES - rows.shape[1])), constant_values=-1)
     vmem = pl.BlockSpec(memory_space=pltpu.VMEM)
     hbm = pl.BlockSpec(memory_space=pl.ANY)
     sem = pltpu.SemaphoreType.DMA
@@ -486,7 +581,7 @@
             jax.ShapeDtypeStruct((ROWS, 512), BF16),
             jax.ShapeDtypeStruct((SESS, NS, CH), F32),
         ),
-        in_specs=[vmem] * 8 + [hbm] * 6,
+        in_specs=[vmem] * 2 + [pl.BlockSpec(memory_space=pltpu.SMEM)] + [vmem] * 7 + [hbm] * 6,
         out_specs=(hbm, hbm),
         scratch_shapes=[
             pltpu.VMEM((16, 2 * CH, LANES), BF16),
@@ -507,6 +602,11 @@
             pltpu.VMEM((16, 1, 2 * HALF), F32),
             pltpu.VMEM((256, HALF), F32),
             pltpu.VMEM((96, 2 * HALF), F32),
+            pltpu.VMEM((SESS * 3 * CB, LANES), F32),
+            pltpu.VMEM((FIX * CB, LANES), F32),
+            pltpu.VMEM((FIX, CH), BF16),
+            pltpu.VMEM((FIX, PW), BF16),
+            pltpu.VMEM((8, FIX, PW), BF16),
             pltpu.VMEM((24 * CB, LANES), F32),
             pltpu.VMEM((LANES, CH), BF16),
             pltpu.VMEM((8 * RB, PW), BF16),
@@ -521,7 +621,8 @@
             pltpu.VMEM((ROWS, 512), BF16),
             sem((6,)), sem((64,)), sem((64,)), sem((2,)), sem((2,)), sem((16,)), sem((16,)),
             sem((16,)), sem((16,)), sem((16,)), sem((16,)), sem((8,)), sem((8,)), sem((8,)), sem((8,)),
-            sem((SESS,)), sem((SESS,)), sem((16,)), sem((8, 2)), sem((SESS + 1,)),
+            sem((8,)), sem((8,)),
+            sem((SESS,)), sem((SESS,)), sem((16, 2)), sem((8, 2, 2)), sem((SESS,)), sem((2, 2)),
         ],
         compiler_params=pltpu.CompilerParams(
             collective_id=0, has_side_effects=True, vmem_limit_bytes=62 << 20
@@ -530,7 +631,8 @@
             flops=2 * ROWS * CH * (4096 + 1056), bytes_accessed=12 << 20, transcendentals=20 << 20
         ),
     )(
-        conv_weight, conv_bias.reshape(1, -1), meta, coupling_weight, step_gain.reshape(1, -1),
+        page_owner, page_slot, page_count,
+        conv_weight, conv_bias.reshape(1, -1), coupling_weight, step_gain.reshape(1, -1),
         step_bias.reshape(1, -1), decay_log, skip_gain.reshape(1, -1),
         conv_input.reshape(ROWS, CH), gate_input.reshape(ROWS, CH), state_pool,
         step_in_weight, step_weight, out_weight,

time: 166 us -> 139 us (0.84)
  Pallas kernels: 158 us -> 133 us
    pallas_call x1, Pallas kernels: 158 us -> 133 us  [body(): pl.pallas_call(kernel, out_shape=(jax.ShapeDtypeStruct((ROWS, 512), BF16)...]
    unnamed x2 -> x3, local copies, waits for them, and re-layouts: 4 us -> 5.41 us
where the time goes in v2:
time: 139 us
  Pallas kernels  133 us (96%)
  local copies, waits for them, and re-layouts  5.41 us (4%)
    pallas_call x1, Pallas kernels, body(): pl.pallas_call(kernel, out_shape=(jax.ShapeDtypeStruct((ROWS, 512), BF16)...  133 us
    unnamed x3, local copies, waits for them, and re-layouts  5.41 us

profile of v2, /device:TPU:5, one launch (start us, length us, event | category | flops | bytes accessed | tf_op | source)
XLA Modules:
  0.0 138.7 jit_solution(11335815138604399657)
XLA Ops:
  0.6 1.4 %copy.18.page_owner = s32[6,16,1]{2,1,0:T(8,128)} copy(s32[6,16,1]{1,2,0:T(1,128)} %param.21) | data formatting | bytes 768 | tf_op args[5]
  2.0 132.7 %shard_map.167 = (bf16[576,512]{1,0:T(8,128)(2,1)}, f32[6,16,2048]{2,1,0:T(8,128)}) custom-call(s32[6,16,1]{2,1,0:T(8,128)} %copy.18.page_owner, s32[6,16]{1,0:T(8,128)} %page_slot.1, s32[6]{0:T(128)} %page_count.1, f32[4,2048]{1,0:T(4,128)} %conv_w.1, f32[1,2048]{1,0:T(1,128)} %bitcast.10, bf16[32,2048]{1,0:T(8,128)(2,1)} %coup_w.1, f32[1,512]{1,0:T(1,128)} %bitcast.13, ...), custom_call_target="tpu_custom_call" | custom-call | flops 12155092992 | bytes 12582912 | tf_op jit(solution)/shard_map/pallas_call | solution.py:578
  134.7 1.9 %copy.21 = bf16[6,96,512]{2,1,0:T(8,128)(2,1)} copy(bf16[6,96,512]{2,1,0:T(8,128)(2,1)} %bitcast.7) | data formatting | bytes 1179648
  136.7 2.1 %copy.22 = f32[6,16,2048]{2,1,0:T(8,128)} copy(f32[6,16,2048]{2,1,0:T(8,128)} %get-tuple-element.9) | data formatting | bytes 1572864

commit v3 on v2

--- a/solution.py
+++ b/solution.py
@@ -16,7 +16,9 @@
 NS, KW, RANK, ENT = 16, 4, 512, 19
 PAGE = CH // CB * ENT
 HALF = 10 * LANES
-RB = 80
+GROUPS = ((0, 4), (4, 6))
+GROUP_ROWS = ((0, 48), (384, 32))
+PADDED = 640
 PW = RANK + LANES
 FIX = 32
 QR = 1024
@@ -95,7 +97,7 @@
     mixer_out, final_state,
     W, G, XN, GN, SIW, SWV, S2, D2, PL, PP, REQ, RQIN, PS, PRV, S8, P8, RALL, FT,
     PRE, F2, XF, FXS, FXR,
-    SPB, CPW, RSS, RSR, AGB, EB, BC, FSB, FSV, OB, RBO, OUTV,
+    SPB, CPW, RSS, RSR, AGB, FXP, EB, BC, FSB, FSV, OB, RBO, OUTV,
     loc_sem, ag_send, ag_recv, sib_send, sib_recv, rq_send, rq_recv,
     pa_send, pa_recv, pb_send, pb_recv, rs_send, rs_recv, an_send, an_recv, fx_send, fx_recv,
     gx_send, gx_recv, ob_send, ob_recv, fs_sem, out_sem,
@@ -262,7 +264,7 @@
         SPB[pl.ds(8 * CB + p, NS, stride=CB), :] = -LOG2E * jnp.exp(decay_log[:, cols])
     CPW[...] = jnp.zeros_like(CPW)
     CPW[0 : 2 * NS, :] = coup_w[...]
-    RSS[ROWS:, :] = jnp.zeros((8 * RB - ROWS, PW), BF16)
+    RSS[ROWS:, :] = jnp.zeros((PADDED - ROWS, PW), BF16)
 
     ld_x.wait()
 
@@ -301,8 +303,6 @@
         lax.fori_loop(0, NEW // 8, step, (none, none, none))
         return 0
 
-    lax.fori_loop(0, SESS, conv_session, 0)
-
     def collect(g, _):
         r = pl.multiple_of(g * 16, 16)
         for p in range(CB):
@@ -311,8 +311,6 @@
             ].astype(BF16)
         return 0
 
-    lax.fori_loop(0, ROWS // 16, collect, 0)
-
     ld_siw.wait()
 
     def project(m, _):
@@ -321,14 +319,31 @@
         RSS[r, RANK:] = dot_nt(XN[r, :], CPW[...]).astype(BF16)
         return 0
 
-    lax.fori_loop(0, ROWS // 96, project, 0)
-    for d in range(1, 8):
-        to = (tn + d) % 8
-        remote(
-            RSS.at[pl.ds(pl.multiple_of(to * RB, 16), RB)], RSR.at[d],
-            rs_send.at[d], rs_recv.at[d], (dp, to),
-        )
+    def prepare(group):
+        first, last = GROUPS[group]
+        lax.fori_loop(first, last, conv_session, 0)
+        lax.fori_loop(first * NEW // 16, last * NEW // 16, collect, 0)
+        lax.fori_loop(first, last, project, 0)
+
+    def share(group, who):
+        base, rows = GROUP_ROWS[group]
+        return pl.ds(pl.multiple_of(base + who * rows, 16), rows)
+
+    def landing(group):
+        return pl.ds(48 * group, GROUP_ROWS[group][1])
+
+    def send_sums(group):
+        for d in range(1, 8):
+            to = (tn + d) % 8
+            remote(
+                RSS.at[share(group, to)], RSR.at[d, landing(group)],
+                rs_send.at[group, d], rs_recv.at[group, d], (dp, to),
+            )
+
+    prepare(0)
+    send_sums(0)
     advance(8)
+    prepare(1)
 
     EB[...] = (iota((LANES, 2 * NS * LANES), 0) == iota((LANES, 2 * NS * LANES), 1) // LANES).astype(
         F32
@@ -378,22 +393,34 @@
         inv_rms = lax.rsqrt(jnp.mean(low * low, axis=-1, keepdims=True) + EPSILON)
         return (low * inv_rms * step_gain[...]).astype(BF16), sums[:, RANK:].astype(BF16)
 
-    mine = pl.ds(pl.multiple_of(tn * RB, 16), RB)
-    total = RSS[mine, :].astype(F32)
-    for d in range(1, 8):
-        arrived(RSR.at[d], rs_send.at[d], rs_recv.at[d])
-        total = total + RSR[d].astype(F32)
-    AGB[mine, 0:RANK], AGB[mine, RANK:] = normalize(total)
-    an_sends = []
-    for d in range(1, 8):
-        to = (tn + d) % 8
-        remote(AGB.at[mine], AGB.at[mine], an_send.at[d], an_recv.at[d], (dp, to), an_sends)
+    an_sends = ([], [])
+
+    def spread_normed(group):
+        mine = share(group, tn)
+        total = RSS[mine, :].astype(F32)
+        for d in range(1, 8):
+            ref = RSR.at[d, landing(group)]
+            arrived(ref, rs_send.at[group, d], rs_recv.at[group, d])
+            total = total + ref[...].astype(F32)
+        AGB[mine, 0:RANK], AGB[mine, RANK:] = normalize(total)
+        for d in range(1, 8):
+            to = (tn + d) % 8
+            remote(
+                AGB.at[mine], AGB.at[mine], an_send.at[group, d], an_recv.at[group, d],
+                (dp, to), an_sends[group],
+            )
+
+    def take_normed(group):
+        for d in range(1, 8):
+            src = (tn + 8 - d) % 8
+            arrived(AGB.at[share(group, src)], an_send.at[group, d], an_recv.at[group, d])
+        for c in an_sends[group]:
+            c.wait_send()
+
+    spread_normed(0)
+    send_sums(1)
     advance(12)
-    for d in range(1, 8):
-        src = (tn + 8 - d) % 8
-        arrived(
-            AGB.at[pl.ds(pl.multiple_of(src * RB, 16), RB)], an_send.at[d], an_recv.at[d]
-        )
+    take_normed(0)
 
     fixed = FXS[...].astype(F32)
     for d in range(1, 8):
@@ -402,15 +429,16 @@
     normed, coupled = normalize(fixed)
     place = iota((96, FIX), 0)
     place = ((place % 16 < 3) & (place // 16 * 3 + place % 16 == iota((96, FIX), 1))).astype(F32)
-    placed = dot(place.astype(BF16), jnp.concatenate([normed, coupled], axis=1))
-    for c in an_sends:
-        c.wait_send()
-    for s in range(SESS):
-        r = slice(s * NEW, s * NEW + 16)
-        AGB[r, :] = jnp.where(
-            iota((16, PW), 0) < 3, placed[s * 16 : s * 16 + 16, :], AGB[r, :].astype(F32)
-        ).astype(BF16)
-
+    FXP[...] = dot(place.astype(BF16), jnp.concatenate([normed, coupled], axis=1))
+
+    def correct(group):
+        for s in range(*GROUPS[group]):
+            r = slice(s * NEW, s * NEW + 16)
+            AGB[r, :] = jnp.where(
+                iota((16, PW), 0) < 3, FXP[s * 16 : s * 16 + 16, :], AGB[r, :].astype(F32)
+            ).astype(BF16)
+
+    correct(0)
     advance(16)
 
     ld_sw.wait()
@@ -425,8 +453,8 @@
                 D2[pl.ds(m * 96 * CB + p + i, 96, stride=CB), :] = v[:, i * LANES : (i + 1) * LANES]
         return 0
 
-    lax.fori_loop(0, ROWS // 96, step_size, 0)
-    advance(20)
+    lax.fori_loop(*GROUPS[0], step_size, 0)
+    advance(18)
 
     def gates(first, last):
         for s in range(first, last):
@@ -466,6 +494,12 @@
     ld_g.wait()
     outs = []
     for s in range(SESS):
+        if s == 1:
+            spread_normed(1)
+        if s == GROUPS[1][0]:
+            take_normed(1)
+            correct(1)
+            lax.fori_loop(*GROUPS[1], step_size, 0)
         both = dot(AGB[s * NEW : (s + 1) * NEW, RANK:], EB[...])
         for n in range(2 * NS):
             BC[n * NEW : (n + 1) * NEW, :] = both[:, n * LANES : (n + 1) * LANES]
@@ -495,7 +529,7 @@
                 return tuple(state)
 
             last = lax.fori_loop(0, NEW // 4, token, start)
-            advance(20 + (5 * (2 * s + h + 1)) // 3)
+            advance(18 + (26 * (2 * s + h + 1)) // 12)
             for n in range(NS):
                 FSB[n * CB + 8 * h : n * CB + 8 * h + 8, :] = last[n]
         for p in range(CB):
@@ -521,6 +555,7 @@
             for pair in PAIRS[:EARLY]:
                 multiply(pair, (0,))
 
+    advance(48)
     gates(SESS // 2, SESS)
     for k, pair in enumerate(PAIRS):
         multiply(pair, (1,) if k < EARLY else (0, 1))
@@ -565,6 +600,24 @@
         c.wait_send()
     for c in outs:
         c.wait()
+
+
+def settle(mixer_in, state_in, mixer_out, state_out, mixer, state, sems):
+    hops = []
+    for i, (src, via, dst) in enumerate(
+        ((state_in, state, state_out), (mixer_in, mixer, mixer_out))
+    ):
+        for s in range(0, SESS, 2):
+            part = pl.ds(s, 2)
+            first = pltpu.make_async_copy(src.at[part], via.at[part], sems.at[0, i, s])
+            last = pltpu.make_async_copy(via.at[part], dst.at[part], sems.at[1, i, s])
+            first.start()
+            hops.append((first, last))
+    for first, last in hops:
+        first.wait()
+        last.start()
+    for first, last in hops:
+        last.wait()
 
 
 def body(
@@ -609,9 +662,10 @@
             pltpu.VMEM((8, FIX, PW), BF16),
             pltpu.VMEM((24 * CB, LANES), F32),
             pltpu.VMEM((LANES, CH), BF16),
-            pltpu.VMEM((8 * RB, PW), BF16),
-            pltpu.VMEM((8, RB, PW), BF16),
-            pltpu.VMEM((8 * RB, PW), BF16),
+            pltpu.VMEM((PADDED, PW), BF16),
+            pltpu.VMEM((8, 80, PW), BF16),
+            pltpu.VMEM((PADDED, PW), BF16),
+            pltpu.VMEM((96, PW), F32),
             pltpu.VMEM((LANES, 2 * NS * LANES), BF16),
             pltpu.VMEM((2 * NS * NEW, LANES), F32),
             pltpu.VMEM((NS * CB, LANES), F32),
@@ -620,8 +674,8 @@
             pltpu.VMEM((8, 2, ROWS, LANES), BF16),
             pltpu.VMEM((ROWS, 512), BF16),
             sem((6,)), sem((64,)), sem((64,)), sem((2,)), sem((2,)), sem((16,)), sem((16,)),
-            sem((16,)), sem((16,)), sem((16,)), sem((16,)), sem((8,)), sem((8,)), sem((8,)), sem((8,)),
-            sem((8,)), sem((8,)),
+            sem((16,)), sem((16,)), sem((16,)), sem((16,)), sem((2, 8)), sem((2, 8)),
+            sem((2, 8)), sem((2, 8)), sem((8,)), sem((8,)),
             sem((SESS,)), sem((SESS,)), sem((16, 2)), sem((8, 2, 2)), sem((SESS,)), sem((2, 2)),
         ],
         compiler_params=pltpu.CompilerParams(
@@ -637,7 +691,19 @@
         conv_input.reshape(ROWS, CH), gate_input.reshape(ROWS, CH), state_pool,
         step_in_weight, step_weight, out_weight,
     )
-    return mixer_out.reshape(SESS, NEW, 512), final_state
+    mixer_out = mixer_out.reshape(SESS, NEW, 512)
+    return pl.pallas_call(
+        settle,
+        out_shape=(
+            jax.ShapeDtypeStruct(mixer_out.shape, BF16),
+            jax.ShapeDtypeStruct(final_state.shape, F32),
+        ),
+        in_specs=[hbm, hbm],
+        out_specs=(hbm, hbm),
+        scratch_shapes=[
+            pltpu.VMEM(mixer_out.shape, BF16), pltpu.VMEM(final_state.shape, F32), sem((2, 2, SESS)),
+        ],
+    )(mixer_out, final_state)
 
 
 def solution(mesh):

time: 139 us -> 127 us (0.914)
  Pallas kernels: 133 us -> 125 us
  local copies, waits for them, and re-layouts: 5.41 us -> 1.41 us
    pallas_call x1, Pallas kernels: 133 us -> 123 us  [body(): pl.pallas_call(kernel, out_shape=(jax.ShapeDtypeStruct((ROWS, 512), BF16)...]
    unnamed x3 -> x1, local copies, waits for them, and re-layouts: 5.41 us -> 1.41 us
    pallas_call x0 -> x1, Pallas kernels: none -> 2.23 us  [body(): pl.pallas_call(settle, out_shape=(jax.ShapeDtypeStruct(mixer_out.shape, B...]
where the time goes in v3:
time: 127 us
  Pallas kernels  125 us (98%)
  local copies, waits for them, and re-layouts  1.41 us (1%)
    pallas_call x1, Pallas kernels, body(): pl.pallas_call(kernel, out_shape=(jax.ShapeDtypeStruct((ROWS, 512), BF16)...  123 us

profile of v3, /device:TPU:5, one launch (start us, length us, event | category | flops | bytes accessed | tf_op | source)
XLA Modules:
  0.0 127.0 jit_solution(4008345962089792840)
XLA Ops:
  0.6 1.4 %copy.18.page_owner = s32[6,16,1]{2,1,0:T(8,128)} copy(s32[6,16,1]{1,2,0:T(1,128)} %param.21) | data formatting | bytes 768 | tf_op args[5]
  2.0 122.5 %shard_map.167 = (bf16[576,512]{1,0:T(8,128)(2,1)}, f32[6,16,2048]{2,1,0:T(8,128)}) custom-call(s32[6,16,1]{2,1,0:T(8,128)} %copy.18.page_owner, s32[6,16]{1,0:T(8,128)} %page_slot.1, s32[6]{0:T(128)} %page_count.1, f32[4,2048]{1,0:T(4,128)} %conv_w.1, f32[1,2048]{1,0:T(1,128)} %bitcast.10, bf16[32,2048]{1,0:T(8,128)(2,1)} %coup_w.1, f32[1,512]{1,0:T(1,128)} %bitcast.13, ...), custom_call_target="tpu_custom_call" | custom-call | flops 12155092992 | bytes 12582912 | tf_op jit(solution)/shard_map/pallas_call | solution.py:631
  124.6 2.2 %shard_map.168 = (bf16[6,96,512]{2,1,0:T(8,128)(2,1)}, f32[6,16,2048]{2,1,0:T(8,128)}) custom-call(bf16[6,96,512]{2,1,0:T(8,128)(2,1)} %bitcast.7, f32[6,16,2048]{2,1,0:T(8,128)} %get-tuple-element.5.state_in), custom_call_target="tpu_custom_call" | custom-call | tf_op jit(solution)/shard_map/pallas_call | solution.py:695

commit v4 on v3

--- a/solution.py
+++ b/solution.py
@@ -51,9 +51,10 @@
 
 PAIRS = (
     ((0, 0), (0, 1)), ((0, 3), (1, 0)), ((3, 0), (2, 0)), ((1, 3), (3, 3)),
-    ((1, 1), (3, 1)), ((0, 2), (2, 1)), ((2, 3), (1, 2)), ((3, 2), (2, 2)),
+    ((1, 1), (3, 1)), ((0, 2), (2, 1)), ((2, 3), (1, 2)), ((3, 2),), ((2, 2),),
 )
-EARLY = 2
+EARLY = {2: (0, 2), 4: (2, 4)}
+SOON = 4
 HROWS = ROWS // 2
 
 
@@ -144,62 +145,19 @@
         pl.semaphore_signal(bar, inc=1, device_id=((dp + d) % 16, tn), device_id_type=MESH)
     for d in range(1, 8):
         pl.semaphore_signal(bar, inc=1, device_id=(dp, (tn + d) % 8), device_id_type=MESH)
-    pl.semaphore_wait(bar, 22)
-
-    def part_rows(q, p):
-        base = own_rows if q == 0 else sib_rows
-        return pl.ds(pl.multiple_of(base + p * QR, QR), QR)
-
-    def dp_of(q, a, b):
-        return a * 4 + b if q == 0 else b * 4 + a
-
-    def coords(q):
-        return (x, z) if q == 0 else (z, x)
-
-    def part(q, da, db, p):
-        a, b = coords(q)
-        return W.at[dp_of(q, (a + 4 - da) % 4, (b + 4 - db) % 4), part_rows(q, p)]
-
-    def gather_step(label):
-        q, da, db, p = label
-        a, b = coords(q)
-        ref = part(q, da, db, p)
-        if (da, db) != (0, 0):
-            k = gather_label(*label)
-            arrived(ref, ag_send.at[k], ag_recv.at[k])
-        elif q == 1:
-            arrived(ref, sib_send.at[p], sib_recv.at[p])
-        for axis, step, nlabel in gather_forwards(*label):
-            k = gather_label(*nlabel)
-            to = ((a + step) % 4, b) if axis == "a" else (a, (b + step) % 4)
-            remote(ref, ref, ag_send.at[k], ag_recv.at[k], (dp_of(q, *to), tn))
-
-    events = gather_events()
-    cursor = [0]
-
-    def advance(upto):
-        while cursor[0] < min(upto, len(events)):
-            gather_step(events[cursor[0]])
-            cursor[0] += 1
-
-    for p in (0, 1):
-        remote(
-            out_w.at[pl.ds(p * QR, QR), pl.ds(sib_lanes, LANES)],
-            W.at[dp, part_rows(0, p)], sib_send.at[p], sib_recv.at[p], (dp, sib),
-        )
 
     row16 = iota((16, LANES), 0)
     lane16 = iota((16, LANES), 1)
-    owner = jnp.zeros((16, LANES), jnp.int32)
     spread16 = (lane16 % 16 == row16).astype(F32).astype(BF16)
-    slot = dot(page_slot[...].astype(F32).astype(BF16), spread16)
-    slot = jnp.where(iota((SESS, LANES), 0) == iota((SESS, LANES), 1) // 16, slot, 0.0)
-    slot = jnp.sum(slot, axis=0, keepdims=True).astype(jnp.int32)
-    for s in range(SESS):
-        here = lane16 == s * 16 + row16
-        owner = jnp.where(here, page_owner[s], owner)
+
+    def along_lanes(listed):
+        wide = dot(listed.astype(F32).astype(BF16), spread16)
+        wide = jnp.where(iota((SESS, LANES), 0) == iota((SESS, LANES), 1) // 16, wide, 0.0)
+        return jnp.sum(wide, axis=0, keepdims=True).astype(jnp.int32)
+
+    slot = along_lanes(page_slot[...])
     lane = iota((1, LANES), 1)
-    owner = jnp.sum(owner.astype(F32), axis=0, keepdims=True).astype(jnp.int32)
+    owner = along_lanes(page_owner[:, 0, :])
     owner = jnp.where(lane < 96, owner, 16)
     count = jnp.zeros((1, LANES), jnp.int32)
     for s in range(SESS):
@@ -215,14 +173,71 @@
     ask = (ask_row == row_io).astype(F32).astype(BF16)
     slot_hot = (iota((LANES, LANES), 0) == slot).astype(F32).astype(BF16)
     REQ[...] = dot_nt(ask, slot_hot).astype(BF16).reshape(16, 16, LANES)
+    for p in range(CB):
+        cols = slice(p * LANES, (p + 1) * LANES)
+        SPB[pl.ds(p, KW, stride=CB), :] = conv_w[:, cols]
+        SPB[pl.ds(4 * CB + p, 1), :] = conv_b[:, cols]
+        SPB[pl.ds(5 * CB + p, 1), :] = skip[:, cols]
+        SPB[pl.ds(8 * CB + p, NS, stride=CB), :] = -LOG2E * jnp.exp(decay_log[:, cols])
+    CPW[...] = jnp.zeros_like(CPW)
+    CPW[0 : 2 * NS, :] = coup_w[...]
+    RSS[ROWS:, :] = jnp.zeros((PADDED - ROWS, PW), BF16)
+
+    EB[...] = (iota((LANES, 2 * NS * LANES), 0) == iota((LANES, 2 * NS * LANES), 1) // LANES).astype(
+        F32
+    ).astype(BF16)
+    pl.semaphore_wait(bar, 22)
+
+    def part_rows(q, p):
+        base = own_rows if q == 0 else sib_rows
+        return pl.ds(pl.multiple_of(base + p * QR, QR), QR)
+
+    def dp_of(q, a, b):
+        return a * 4 + b if q == 0 else b * 4 + a
+
+    def coords(q):
+        return (x, z) if q == 0 else (z, x)
+
+    def part(q, da, db, p):
+        a, b = coords(q)
+        return W.at[dp_of(q, (a + 4 - da) % 4, (b + 4 - db) % 4), part_rows(q, p)]
+
+    def gather_step(label):
+        q, da, db, p = label
+        a, b = coords(q)
+        ref = part(q, da, db, p)
+        if (da, db) != (0, 0):
+            k = gather_label(*label)
+            arrived(ref, ag_send.at[k], ag_recv.at[k])
+        elif q == 1:
+            arrived(ref, sib_send.at[p], sib_recv.at[p])
+        for axis, step, nlabel in gather_forwards(*label):
+            k = gather_label(*nlabel)
+            to = ((a + step) % 4, b) if axis == "a" else (a, (b + step) % 4)
+            remote(ref, ref, ag_send.at[k], ag_recv.at[k], (dp_of(q, *to), tn))
+
+    events = gather_events()
+    cursor = [0]
+
+    def advance(upto):
+        while cursor[0] < min(upto, len(events)):
+            gather_step(events[cursor[0]])
+            cursor[0] += 1
+
+    for p in (0, 1):
+        remote(
+            out_w.at[pl.ds(p * QR, QR), pl.ds(sib_lanes, LANES)],
+            W.at[dp, part_rows(0, p)], sib_send.at[p], sib_recv.at[p], (dp, sib),
+        )
+
     RQIN[dp] = REQ[dp]
     for d in range(1, 16):
         to = (dp + d) % 16
         remote(REQ.at[to], RQIN.at[dp], rq_send.at[d], rq_recv.at[d], (to, tn))
+    ld_w.wait()
+    advance(2)
     got = (got_row == row_io).astype(F32).T[0:96, :].astype(BF16)
 
-    ld_w.wait()
-    advance(1)
 
     ld_pool.wait()
     pool_low = PL[...].astype(BF16)
@@ -256,16 +271,6 @@
 
     advance(4)
 
-    for p in range(CB):
-        cols = slice(p * LANES, (p + 1) * LANES)
-        SPB[pl.ds(p, KW, stride=CB), :] = conv_w[:, cols]
-        SPB[pl.ds(4 * CB + p, 1), :] = conv_b[:, cols]
-        SPB[pl.ds(5 * CB + p, 1), :] = skip[:, cols]
-        SPB[pl.ds(8 * CB + p, NS, stride=CB), :] = -LOG2E * jnp.exp(decay_log[:, cols])
-    CPW[...] = jnp.zeros_like(CPW)
-    CPW[0 : 2 * NS, :] = coup_w[...]
-    RSS[ROWS:, :] = jnp.zeros((PADDED - ROWS, PW), BF16)
-
     ld_x.wait()
 
     def spread(g, _):
@@ -345,9 +350,6 @@
     advance(8)
     prepare(1)
 
-    EB[...] = (iota((LANES, 2 * NS * LANES), 0) == iota((LANES, 2 * NS * LANES), 1) // LANES).astype(
-        F32
-    ).astype(BF16)
     advance(8)
 
     for d in range(1, 16):
@@ -365,7 +367,7 @@
 
     advance(8)
 
-    F2[SESS * 3 * CB :, :] = jnp.zeros(((FIX - SESS * 3) * CB, LANES), F32)
+    F2[SESS * 3 * CB : FIX * CB, :] = jnp.zeros(((FIX - SESS * 3) * CB, LANES), F32)
     for s in range(SESS):
         hist = [
             FT[s * CB : (s + 1) * CB, (NS + w) * LANES : (NS + w + 1) * LANES] for w in range(3)
@@ -513,8 +515,8 @@
 
             def token(i, state, h=h, s=s, rate=rate, direct=direct):
                 state = list(state)
-                for u in range(4):
-                    t = i * 4 + u
+                for u in range(8):
+                    t = i * 8 + u
                     at = pl.ds(pl.multiple_of((s * NEW + t) * CB + 8 * h, 8), 8)
                     dt, sg = D2[at, :], S2[at, :]
                     dx = dt * sg
@@ -528,8 +530,8 @@
                     S2[at, :] = acc[0] + acc[1]
                 return tuple(state)
 
-            last = lax.fori_loop(0, NEW // 4, token, start)
-            advance(18 + (26 * (2 * s + h + 1)) // 12)
+            last = lax.fori_loop(0, NEW // 8, token, start)
+            advance(18 + (22 * (2 * s + h + 1)) // 12)
             for n in range(NS):
                 FSB[n * CB + 8 * h : n * CB + 8 * h + 8, :] = last[n]
         for p in range(CB):
@@ -550,15 +552,16 @@
         lax.fori_loop(0, NEW // 16, gate, 0)
         here = G.at[core, pl.ds(s * NEW, NEW)]
         remote(here, here, gx_send.at[s], gx_recv.at[s], (dp, sib))
-        if s == SESS // 2 - 1:
-            gates(0, s + 1)
-            for pair in PAIRS[:EARLY]:
+        if s in EARLY:
+            if s == SESS // 2 - 1:
+                gates(0, s + 1)
+            for pair in PAIRS[slice(*EARLY[s])]:
                 multiply(pair, (0,))
 
     advance(48)
     gates(SESS // 2, SESS)
     for k, pair in enumerate(PAIRS):
-        multiply(pair, (1,) if k < EARLY else (0, 1))
+        multiply(pair, (1,) if k < SOON else (0, 1))
     advance(len(events))
 
     for side in (1 - z % 2, z % 2):
@@ -643,8 +646,8 @@
             pltpu.VMEM((ROWS, CH), BF16),
             pltpu.VMEM((CH, RANK), BF16),
             pltpu.VMEM((RANK, CH), BF16),
-            pltpu.VMEM((ROWS * CB, LANES), F32),
-            pltpu.VMEM((ROWS * CB, LANES), F32),
+            pltpu.VMEM((ROWS * CB + 16, LANES), F32),
+            pltpu.VMEM((ROWS * CB + 16, LANES), F32),
             pltpu.VMEM((LANES, PAGE), F32),
             pltpu.VMEM((LANES, 2 * HALF), BF16),
             pltpu.VMEM((16, 16, LANES), BF16),
@@ -656,19 +659,19 @@
             pltpu.VMEM((256, HALF), F32),
             pltpu.VMEM((96, 2 * HALF), F32),
             pltpu.VMEM((SESS * 3 * CB, LANES), F32),
-            pltpu.VMEM((FIX * CB, LANES), F32),
+            pltpu.VMEM((FIX * CB + 16, LANES), F32),
             pltpu.VMEM((FIX, CH), BF16),
             pltpu.VMEM((FIX, PW), BF16),
             pltpu.VMEM((8, FIX, PW), BF16),
-            pltpu.VMEM((24 * CB, LANES), F32),
+            pltpu.VMEM((24 * CB + 16, LANES), F32),
             pltpu.VMEM((LANES, CH), BF16),
             pltpu.VMEM((PADDED, PW), BF16),
             pltpu.VMEM((8, 80, PW), BF16),
             pltpu.VMEM((PADDED, PW), BF16),
             pltpu.VMEM((96, PW), F32),
             pltpu.VMEM((LANES, 2 * NS * LANES), BF16),
-            pltpu.VMEM((2 * NS * NEW, LANES), F32),
-            pltpu.VMEM((NS * CB, LANES), F32),
+            pltpu.VMEM((2 * NS * NEW + 8, LANES), F32),
+            pltpu.VMEM((NS * CB + 16, LANES), F32),
             pltpu.VMEM((SESS, NS, CH), F32),
             pltpu.VMEM((16, ROWS, LANES), BF16),
             pltpu.VMEM((8, 2, ROWS, LANES), BF16),
@@ -685,7 +688,7 @@
             flops=2 * ROWS * CH * (4096 + 1056), bytes_accessed=12 << 20, transcendentals=20 << 20
         ),
     )(
-        page_owner, page_slot, page_count,
+        jnp.transpose(page_owner, (0, 2, 1)), page_slot, page_count,
         conv_weight, conv_bias.reshape(1, -1), coupling_weight, step_gain.reshape(1, -1),
         step_bias.reshape(1, -1), decay_log, skip_gain.reshape(1, -1),
         conv_input.reshape(ROWS, CH), gate_input.reshape(ROWS, CH), state_pool,

time: 127 us -> 123 us (0.969)
  Pallas kernels: 125 us -> 122 us
  local copies, waits for them, and re-layouts: 1.41 us -> 0 us
    pallas_call x1, Pallas kernels: 123 us -> 119 us  [body(): pl.pallas_call(kernel, out_shape=(jax.ShapeDtypeStruct((ROWS, 512), BF16)...]
    unnamed x1 -> x0, local copies, waits for them, and re-layouts: 1.41 us -> none
where the time goes in v4:
time: 123 us; the launch traced here: 122 us
  Pallas kernels  122 us (99%)
    pallas_call x1, Pallas kernels, body(): pl.pallas_call(kernel, out_shape=(jax.ShapeDtypeStruct((ROWS, 512), BF16)...  119 us

profile of v4, /device:TPU:5, one launch (start us, length us, event | category | flops | bytes accessed | tf_op | source)
XLA Modules:
  0.0 122.4 jit_solution(5014144567112911059)
XLA Ops:
  0.6 119.4 %shard_map.167 = (bf16[576,512]{1,0:T(8,128)(2,1)}, f32[6,16,2048]{2,1,0:T(8,128)}) custom-call(s32[6,1,16]{2,1,0:T(1,128)} %bitcast.14, s32[6,16]{1,0:T(8,128)} %page_slot.1, s32[6]{0:T(128)} %page_count.1, f32[4,2048]{1,0:T(4,128)} %conv_w.1, f32[1,2048]{1,0:T(1,128)} %bitcast.11, bf16[32,2048]{1,0:T(8,128)(2,1)} %coup_w.1, f32[1,512]{1,0:T(1,128)} %bitcast.15, ...), custom_call_target="tpu_custom_call" | custom-call | flops 12155092992 | bytes 12582912 | tf_op jit(solution)/shard_map/pallas_call | solution.py:634
  120.0 2.2 %shard_map.168 = (bf16[6,96,512]{2,1,0:T(8,128)(2,1)}, f32[6,16,2048]{2,1,0:T(8,128)}) custom-call(bf16[6,96,512]{2,1,0:T(8,128)(2,1)} %bitcast.8, f32[6,16,2048]{2,1,0:T(8,128)} %get-tuple-element.5.state_in), custom_call_target="tpu_custom_call" | custom-call | tf_op jit(solution)/shard_map/pallas_call | solution.py:698

commit v5 on v4

--- a/solution.py
+++ b/solution.py
@@ -558,7 +558,7 @@
             for pair in PAIRS[slice(*EARLY[s])]:
                 multiply(pair, (0,))
 
-    advance(48)
+    advance(50)
     gates(SESS // 2, SESS)
     for k, pair in enumerate(PAIRS):
         multiply(pair, (1,) if k < SOON else (0, 1))

time: 123 us -> 124 us (level)
    pallas_call x1, Pallas kernels: 119 us -> 121 us  [body(): pl.pallas_call(kernel, out_shape=(jax.ShapeDtypeStruct((ROWS, 512), BF16)...]
where the time goes in v5:
time: 124 us
  Pallas kernels  123 us (99%)
    pallas_call x1, Pallas kernels, body(): pl.pallas_call(kernel, out_shape=(jax.ShapeDtypeStruct((ROWS, 512), BF16)...  121 us

profile of v5, /device:TPU:5, one launch (start us, length us, event | category | flops | bytes accessed | tf_op | source)
XLA Modules:
  0.0 124.0 jit_solution(2397951732752042351)
XLA Ops:
  0.6 121.0 %shard_map.167 = (bf16[576,512]{1,0:T(8,128)(2,1)}, f32[6,16,2048]{2,1,0:T(8,128)}) custom-call(s32[6,1,16]{2,1,0:T(1,128)} %bitcast.14, s32[6,16]{1,0:T(8,128)} %page_slot.1, s32[6]{0:T(128)} %page_count.1, f32[4,2048]{1,0:T(4,128)} %conv_w.1, f32[1,2048]{1,0:T(1,128)} %bitcast.11, bf16[32,2048]{1,0:T(8,128)(2,1)} %coup_w.1, f32[1,512]{1,0:T(1,128)} %bitcast.15, ...), custom_call_target="tpu_custom_call" | custom-call | flops 12155092992 | bytes 12582912 | tf_op jit(solution)/shard_map/pallas_call | solution.py:634
  121.6 2.2 %shard_map.168 = (bf16[6,96,512]{2,1,0:T(8,128)(2,1)}, f32[6,16,2048]{2,1,0:T(8,128)}) custom-call(bf16[6,96,512]{2,1,0:T(8,128)(2,1)} %bitcast.8, f32[6,16,2048]{2,1,0:T(8,128)} %get-tuple-element.5.state_in), custom_call_target="tpu_custom_call" | custom-call | tf_op jit(solution)/shard_map/pallas_call | solution.py:698
